TPU v7x, 256 devices: a whole 4x4x8 slice. The times are simulated.
256 devices in a mesh: grp: 4 (over z_lo, core), dev: 64 (over y, z_hi, x).
Axes of the slice: x: 4, y: 4, z: 8 (z_hi: 4, z_lo: 2; z = z_hi * 2 + z_lo), core: 2. Of those that a mesh axis runs over, the one named last changes fastest.
Arguments:
- field: bfloat16 [1024, 222, 4096], P(('grp', 'dev')), may hold values from -6 to 6
- level_start: float32 [222, 48], replicated, may hold values from -0.375 to 0.375
- time_start: float32 [768, 128], replicated, may hold values from -0.21875 to 0.21875
- lag_offsets: int32 [8], replicated, may hold values from 0 to 256, as said below
Outputs:
- level_basis: float32 [222, 48], replicated
- low_rank: float32 [768, 768], replicated
Inputs may be any that keep to these rules, and one draw needn't show every extreme that they name: `lag_offsets`: the first offset is 0 and the last is 256; offsets are distinct.
All inputs are finite; a program needn't handle non-finite values.
Results may differ from a plain program's by a relative error of at most 0.0014.
The roundings to bfloat16 on the way count: a program that leaves them out, or rounds other values in their place, can miss the bound.
Values may be sent and summed in bfloat16 or wider, within the bound.
No kernel may reach another device: no remote copies, remote signals or barrier semaphores. Data moves between devices by JAX's collectives and lax.ppermute only.
A program may use at most 128 MiB of HBM per device.

v0:
```python
import functools
import jax
import jax.numpy as jnp
from jax import lax
from jax.experimental import pallas as pl
from jax.experimental.pallas import tpu as pltpu
from jax.sharding import Mesh, PartitionSpec as P

AXES = ("zl", "co", "y", "zh", "x")
SIZES = (2, 2, 4, 4, 4)
HIGH = lax.Precision.HIGHEST
LANES = 128
ITERS = 3

def dot(a, b, dims=((1,), (0,)), precision=HIGH):
    return lax.dot_general(a, b, (dims, ((), ())), precision=precision, preferred_element_type=jnp.float32)


def split(x):
    hi = x.astype(jnp.bfloat16)
    rest = x - hi.astype(jnp.float32)
    mid = rest.astype(jnp.bfloat16)
    low = (rest - mid.astype(jnp.float32)).astype(jnp.bfloat16)
    return hi, mid, low


def across(row):
    return jnp.broadcast_to(row, (8, LANES))


def inverse_cholesky(gram, out_ref):
    n = gram.shape[0]
    tiles = n // 8
    lane = lax.broadcasted_iota(jnp.int32, (8, LANES), 1)
    sub = lax.broadcasted_iota(jnp.int32, (8, LANES), 0)
    left = [gram[8 * t : 8 * t + 8, :] for t in range(tiles)]
    right = [jnp.where(lane == sub + 8 * t, 1.0, 0.0) for t in range(tiles)]
    for i in range(0, n, 4):
        here, off = i // 8, i % 8
        cols = [
            {t: jnp.broadcast_to(left[t][:, i + k : i + k + 1], (8, LANES)) for t in range(here, tiles)}
            for k in range(4)
        ]
        entry = lambda r, k: across(cols[k][here][off + r : off + r + 1, :])
        low, inv = {}, []
        for k in range(4):
            for r in range(k, 4):
                v = entry(r, k)
                for q in range(k):
                    v = v - low[r, q] * low[k, q]
                if r == k:
                    inv.append(lax.rsqrt(v))
                else:
                    low[r, k] = v * inv[k]
        rows = []
        for k in range(4):
            a = across(left[here][off + k : off + k + 1, :])
            b = across(right[here][off + k : off + k + 1, :])
            for q in range(k):
                a = a - low[k, q] * rows[q][0]
                b = b - low[k, q] * rows[q][1]
            rows.append((a * inv[k], b * inv[k]))
            out_ref[i + k : i + k + 1, :] = rows[k][1][0:1, :]
        for t in range(here + (off > 0), tiles):
            mult = []
            for k in range(4):
                v = cols[k][t]
                for q in range(k):
                    v = v - mult[q] * low[k, q]
                mult.append(v * inv[k])
            for k in range(4):
                left[t] = left[t] - mult[k] * rows[k][0]
                right[t] = right[t] - mult[k] * rows[k][1]


def truncate_kernel(core_ref, mine_ref, other_ref, start_ref, out_ref, d_ref, half_ref, split_ref, z_ref, w_ref, linv_ref):
    each, high, _ = mine_ref.shape
    width = d_ref.shape[0]
    for ref, core in ((mine_ref, core_ref[0]), (other_ref, 1 - core_ref[0])):
        for k in range(each):
            half_ref[pl.ds(pl.multiple_of((core * each + k) * high, 8), high), :] = ref[k]
    blocks = width // LANES
    for i in range(blocks):
        for d in range(4):
            j = (i + d) % blocks
            block = half_ref[LANES * i : LANES * (i + 1), LANES * d : LANES * (d + 1)]
            d_ref[LANES * i : LANES * (i + 1), LANES * j : LANES * (j + 1)] = block
            if d in (1, 2):
                d_ref[LANES * j : LANES * (j + 1), LANES * i : LANES * (i + 1)] = block.T
    lagged = d_ref[...]
    rows = jnp.sum(lagged, axis=1, keepdims=True) * (1.0 / width)
    cols = jnp.sum(lagged, axis=0, keepdims=True) * (1.0 / width)
    mean = jnp.sum(rows, axis=0, keepdims=True) * (1.0 / width)
    debiased = lagged - rows - cols + mean
    for k, part in enumerate(split(debiased)):
        split_ref[k] = part

    def times(x):
        n = x.shape[0]
        parts = jnp.concatenate(split(x), axis=0)
        by = lambda m, k: dot(parts[: m * n], split_ref[k], precision=None)
        one, two, three = by(3, 0), by(2, 1), by(1, 2)
        small = one[2 * n :] + two[n:] + three
        return one[:n] + ((one[n : 2 * n] + two[:n]) + small)

    z_ref[...] = times(start_ref[...].T)

    def step(_, carry):
        z = z_ref[...]
        inverse_cholesky(dot(z, z, ((1,), (1,))), linv_ref)
        w_ref[...] = times(z)
        @pl.when(_ < ITERS - 1)
        def _more():
            z_ref[...] = dot(linv_ref[...], w_ref[...])
        return carry

    lax.fori_loop(0, ITERS, step, 0)
    linv = linv_ref[...]
    basis = dot(linv, z_ref[...])
    inner = dot(dot(linv, w_ref[...]), basis, ((1,), (1,)))
    out_ref[...] = dot(basis, dot(inner, basis), ((0,), (0,)))


def truncate(core, mine, other, start):
    width, rank = start.shape
    f32 = jnp.float32
    vm = pl.BlockSpec(memory_space=pltpu.VMEM)
    return pl.pallas_call(
        truncate_kernel,
        out_shape=jax.ShapeDtypeStruct((width, width), f32),
        in_specs=[pl.BlockSpec(memory_space=pltpu.SMEM), vm, vm, vm],
        out_specs=vm,
        scratch_shapes=[
            pltpu.VMEM((width, width), f32),
            pltpu.VMEM((width, 4 * LANES), f32),
            pltpu.VMEM((3, width, width), jnp.bfloat16),
            pltpu.VMEM((rank, width), f32),
            pltpu.VMEM((rank, width), f32),
            pltpu.VMEM((rank, rank), f32),
        ],
        compiler_params=pltpu.CompilerParams(vmem_limit_bytes=48 * 2**20),
        name="truncate",
    )(core, mine, other, start)


def counted(shape, axis):
    return lax.broadcasted_iota(jnp.int32, shape, axis)


def spread(levels, hours, turned=False):
    if turned:
        place, level = counted((levels * hours, 1), 0), counted((1, levels), 1)
    else:
        place, level = counted((1, levels * hours), 1), counted((levels, 1), 0)
    first = level * hours
    return jnp.where((place >= first) & (place < first + hours), 1.0, 0.0).astype(jnp.bfloat16)


def same(rows, columns, of):
    return of(counted((rows, 1), 0)) == of(counted((1, columns), 1))


def level_gram_kernel(scale, core_ref, field_ref, start_ref, out_ref, flat_ref, acc_ref):
    step = pl.program_id(0)
    levels, hours, chunk = field_ref.shape
    total = levels * hours
    tile = 256

    @pl.when(step == 0)
    def _():
        acc_ref[...] = jnp.zeros_like(acc_ref)

    flat = field_ref[...].reshape(total, chunk)
    flat_ref[...] = flat
    for j in range(0, total, tile):
        wide = min(tile, total - j)
        acc_ref[j:, j : j + wide] += dot(flat[j:], flat[j : j + wide], ((1,), (1,)), None)

    @pl.when(step == pl.num_programs(0) - 1)
    def _():
        weight = jnp.where(same(total, total, lambda i: lax.div(i, tile)), 0.5, 1.0)
        weight = jnp.where(same(total, total, lambda i: lax.rem(i, hours)), weight, 0.0)
        half = acc_ref[...] * weight
        left = spread(levels, hours)
        right = spread(levels, hours, True)
        over = sum(dot(left, part, precision=None) for part in reversed(split(half)))
        gram = sum(dot(part, right, precision=None) for part in reversed(split(over)))
        z = (dot(start_ref[...], gram) + dot(start_ref[...], gram, ((1,), (1,)))) * scale
        part = out_ref.shape[1]
        for c in range(2):
            out_ref[lax.bitwise_xor(c, core_ref[0])] = z[part * c : part * (c + 1)]


def level_product(core, field, start, scale):
    levels, hours, columns = field.shape
    nmodes = start.shape[0]
    chunk = 1024
    return pl.pallas_call(
        functools.partial(level_gram_kernel, scale),
        grid=(columns // chunk,),
        out_shape=(
            jax.ShapeDtypeStruct((2, nmodes // 2, levels), jnp.float32),
            jax.ShapeDtypeStruct((levels * hours, columns), jnp.bfloat16),
        ),
        in_specs=[
            pl.BlockSpec(memory_space=pltpu.SMEM),
            pl.BlockSpec((levels, hours, chunk), lambda c: (0, 0, c)),
            pl.BlockSpec((nmodes, levels), lambda c: (0, 0)),
        ],
        out_specs=(
            pl.BlockSpec((2, nmodes // 2, levels), lambda c: (0, 0, 0)),
            pl.BlockSpec((levels * hours, chunk), lambda c: (0, c)),
        ),
        scratch_shapes=[pltpu.VMEM((levels * hours, levels * hours), jnp.float32)],
        compiler_params=pltpu.CompilerParams(vmem_limit_bytes=60 * 2**20),
        name="level_product",
    )(core, field, start)


def project_kernel(hours, core_ref, mine_ref, other_ref, flat_ref, basis_ref, out_ref, weight_ref, linv_ref, z_ref):
    total, chunk = flat_ref.shape
    nmodes, levels = z_ref.shape
    f32, bf16 = jnp.float32, jnp.bfloat16

    @pl.when(pl.program_id(0) == 0)
    def _():
        part = nmodes // 2
        z_ref[pl.ds(pl.multiple_of(part * core_ref[0], 8), part), :] = mine_ref[...]
        z_ref[pl.ds(pl.multiple_of(part * (1 - core_ref[0]), 8), part), :] = other_ref[...]
        z = z_ref[...]
        gram = dot(z, z, ((1,), (1,)))
        padded = jnp.concatenate([gram, jnp.zeros((nmodes, LANES - nmodes), f32)], axis=1)
        inverse_cholesky(padded, linv_ref)
        basis = dot(linv_ref[:, :nmodes], z)
        basis_ref[...] = basis
        modes_by_hours = spread(nmodes, hours, True)
        tall = dot(modes_by_hours, basis.astype(bf16), precision=None).astype(bf16)
        wide = dot(tall, spread(levels, hours), precision=None)
        weight_ref[...] = jnp.where(same(*wide.shape, lambda i: lax.rem(i, hours)), wide, 0.0).astype(bf16)

    made = dot(weight_ref[...], flat_ref[...], precision=None)
    groups, blocks, rows, _ = out_ref.shape
    for a in range(groups):
        for b in range(blocks):
            out_ref[a, b] = made[rows * a : rows * (a + 1), LANES * b : LANES * (b + 1)].astype(bf16)


def project(core, mine, other, flat, hours, groups):
    total, columns = flat.shape
    part, levels = mine.shape
    nmodes = 2 * part
    chunk = 1024
    rows = hours * nmodes // groups
    return pl.pallas_call(
        functools.partial(project_kernel, hours),
        grid=(columns // chunk,),
        out_shape=(
            jax.ShapeDtypeStruct((nmodes, levels), jnp.float32),
            jax.ShapeDtypeStruct((groups, columns // LANES, rows, LANES), jnp.bfloat16),
        ),
        in_specs=[
            pl.BlockSpec(memory_space=pltpu.SMEM),
            pl.BlockSpec((part, levels), lambda c: (0, 0)),
            pl.BlockSpec((part, levels), lambda c: (0, 0)),
            pl.BlockSpec((total, chunk), lambda c: (0, c)),
        ],
        out_specs=(
            pl.BlockSpec((nmodes, levels), lambda c: (0, 0)),
            pl.BlockSpec((groups, chunk // LANES, rows, LANES), lambda c: (0, c, 0, 0)),
        ),
        scratch_shapes=[
            pltpu.VMEM((hours * nmodes, total), jnp.bfloat16),
            pltpu.VMEM((nmodes, LANES), jnp.float32),
            pltpu.VMEM((nmodes, levels), jnp.float32),
        ],
        compiler_params=pltpu.CompilerParams(vmem_limit_bytes=60 * 2**20),
        name="project",
    )(core, mine, other, flat)


def hour_gram_kernel(scale, core_ref, lag_ref, got_ref, out_ref, flat_ref, gram_ref, half_ref):
    senders, rows, _ = got_ref.shape
    width = half_ref.shape[0]
    f32, bf16 = jnp.float32, jnp.bfloat16
    hours = flat_ref.shape[0] // senders
    per = rows // hours
    many = 32
    size = many * rows
    new = counted((size, 1), 0)
    span = many * hours
    mode, rest = lax.div(new, span), lax.rem(new, span)
    wanted = lax.div(rest, hours) * rows + mode * hours + lax.rem(rest, hours)
    pick = jnp.where(counted((1, size), 1) == wanted, 1.0, 0.0).astype(bf16)
    for s in range(0, senders, 2 * many):
        pair = [got_ref[s + many * k : s + many * (k + 1)].reshape(size, LANES) for k in range(2)]
        moved = dot(pick, jnp.concatenate(pair, axis=1), precision=None).astype(bf16)
        for k in range(2):
            for m in range(per):
                flat_ref[hours * s + span * k : hours * s + span * (k + 1), LANES * m : LANES * (m + 1)] = moved[
                    span * m : span * (m + 1), LANES * k : LANES * (k + 1)
                ]
    for i in range(0, flat_ref.shape[0], 256):
        band = dot(flat_ref[i : i + 256, :], flat_ref[...], ((1,), (1,)), None)
        for b in range(gram_ref.shape[0]):
            gram_ref[b, i : i + 256, :] = band[:, LANES * b : LANES * (b + 1)]

    blocks = width // LANES
    lane = lax.broadcasted_iota(jnp.int32, (LANES, LANES), 1)
    for i in range(blocks):
        wanted = [(i + d) % blocks for d in range(4)]

        def add(j, acc):
            offset = lag_ref[j]
            whole, part = lax.div(offset, LANES), lax.rem(offset, LANES)
            turn = lax.rem(LANES - part, LANES)
            at = offset + LANES * i
            load = {}
            for b in sorted(set(wanted) | {w + 1 for w in wanted}):
                column = jnp.minimum(whole + b, gram_ref.shape[0] - 1)
                load[b] = pltpu.roll(gram_ref[column, pl.ds(at, LANES), :], turn, 1)
            return tuple(a + jnp.where(lane < LANES - part, load[w], load[w + 1]) for a, w in zip(acc, wanted))

        acc = lax.fori_loop(0, lag_ref.shape[0], add, tuple(jnp.zeros((LANES, LANES), f32) for _ in wanted))
        for d in range(4):
            half_ref[LANES * i : LANES * (i + 1), LANES * d : LANES * (d + 1)] = acc[d] * scale
    _, each, high, _ = out_ref.shape
    for c in range(2):
        for k in range(each):
            at = (c * each + k) * high
            out_ref[lax.bitwise_xor(c, core_ref[0]), k] = half_ref[at : at + high, :]


def hour_gram(core, lags, got, width, hours, scale):
    senders, rows, _ = got.shape
    total = senders * hours
    wide = 4 * LANES
    smem, vm = pl.BlockSpec(memory_space=pltpu.SMEM), pl.BlockSpec(memory_space=pltpu.VMEM)
    return pl.pallas_call(
        functools.partial(hour_gram_kernel, scale),
        out_shape=jax.ShapeDtypeStruct((2, 16, width // 32, wide), jnp.float32),
        in_specs=[smem, smem, vm],
        out_specs=vm,
        scratch_shapes=[
            pltpu.VMEM((total, rows // hours * LANES), jnp.bfloat16),
            pltpu.VMEM((total // LANES, total, LANES), jnp.float32),
            pltpu.VMEM((width, wide), jnp.float32),
        ],
        compiler_params=pltpu.CompilerParams(vmem_limit_bytes=48 * 2**20),
        name="hour_gram",
    )(core, lags, got)


PLANE = ("y", "x")
COLUMN = ("zl", "zh")


def other_core(x):
    return lax.ppermute(x, "co", [(0, 1), (1, 0)])


def exchange(x, axes):
    return lax.all_to_all(x, axes, split_axis=0, concat_axis=0, tiled=True)


def collect(x, axes):
    return exchange(jnp.broadcast_to(x, (lax.axis_size(axes),) + x.shape), axes)


def sum_over(x, axes):
    return jnp.sum(collect(x, axes), axis=0)


def sum_pieces(pieces):
    here = pieces[0] + other_core(pieces[1])
    mine = jnp.sum(exchange(here, PLANE), axis=0)
    return collect(sum_over(mine, COLUMN), PLANE)


def body(field, level_start, time_start, lag_offsets):
    hour_count, levels, columns = field.shape
    devices = lax.axis_size(AXES)
    hours_all = hour_count * devices
    width = time_start.shape[0]
    nmodes = level_start.shape[1]
    core = lax.axis_index("co").reshape(1)
    scale = 1.0 / (hours_all * columns)
    halves, level_hours = level_product(core, jnp.transpose(field, (1, 0, 2)), level_start.T, scale)
    z = halves[0] + other_core(halves[1])
    z = sum_over(sum_over(z, PLANE), COLUMN)
    level_basis, sent = project(core, z, other_core(z), level_hours, hour_count, 8)
    sent = sent.reshape(devices, 24, LANES)
    received = exchange(sent, AXES)
    scale = 1.0 / (lag_offsets.shape[0] * nmodes * columns)
    summed = sum_pieces(hour_gram(core, lag_offsets, received, width, hour_count, scale))
    low_rank = truncate(core, summed, other_core(summed), time_start)
    return (level_basis.T, low_rank)


def solution(mesh):
    fine = Mesh(mesh.devices.reshape(SIZES), AXES)
    return jax.shard_map(
        body,
        mesh=fine,
        in_specs=(P(AXES, None, None), P(), P(), P()),
        out_specs=(P(), P()),
        check_vma=False,
    )
```

profile of v0, /device:TPU:1, one launch (start us, length us, event | category | flops | bytes accessed | tf_op | source)
XLA Modules:
  0.0 205.4 jit_solution(10389144961726374178)
XLA Ops:
  0.6 12.8 %level_product.1 = (f32[2,24,222]{2,1,0:T(8,128)}, bf16[888,4096]{1,0:T(8,128)(2,1)}) custom-call(s32[1]{0:T(128)} %bitcast.core_ref, bf16[222,4,4096]{2,1,0:T(4,128)(2,1)} %bitcast.15, f32[48,222]{1,0:T(8,128)} %bitcast.17), custom_call_target="tpu_custom_call" | custom-call | tf_op jit(solution)/shard_map/level_product/pallas_call | solution.py:198
  13.4 0.7 slice_bitcast_fusion.2
  14.1 3.3 %collective-permute-start = (f32[24,222]{1,0:T(8,128)S(1)}, f32[24,222]{1,0:T(8,128)S(1)}, u32[]{:S(2)}, u32[]{:S(2)}) collective-permute-start(f32[24,222]{1,0:T(8,128)S(1)} %slice_bitcast_fusion.2), channel_id=1, source_target_pairs={{0,64},{64,0},{1,65},{65,1},{2,66},{66,2},{3,67},{67,3},{4,68},{68... | collective-permute-start | bytes 63944 | tf_op jit(solution)/shard_map/ppermute | solution.py:358
  17.4 0.8 collective-permute-done
  18.2 0.7 bitcast_add_fusion
  19.0 14.4 %all_to_all.30 = f32[16,24,222]{2,1,0:T(8,128)S(1)} all-to-all(f32[16,24,222]{2,1,0:T(8,128)S(1)} %broadcast_in_dim.12), channel_id=1, replica_groups=mesh['zl'=2,'co'=2,'y'=4,'zh'=4,'x'=4] {'y','x'}, dimensions={0} | all-to-all | bytes 681984 | tf_op jit(solution)/shard_map/all_to_all | solution.py:362
  33.4 15.4 %all_to_all.31 = f32[8,24,222]{2,1,0:T(8,128)S(1)} all-to-all(f32[8,24,222]{2,1,0:T(8,128)S(1)} %broadcast_in_dim.13), channel_id=1, replica_groups=mesh['zl'=2,'co'=2,'y'=4,'zh'=4,'x'=4] {'zl','zh'}, dimensions={0} | all-to-all | bytes 340992 | tf_op jit(solution)/shard_map/all_to_all | solution.py:362
  48.8 0.0 copy-start.2
  48.9 2.8 %collective-permute-start.1 = (f32[24,222]{1,0:T(8,128)S(1)}, f32[24,222]{1,0:T(8,128)S(1)}, u32[]{:S(2)}, u32[]{:S(2)}) collective-permute-start(f32[24,222]{1,0:T(8,128)S(1)} %reduce_sum.37.mine_ref), channel_id=1, source_target_pairs={{0,64},{64,0},{1,65},{65,1},{2,66},{66,2},{3,67},{67,3},{4,68},{68... | collective-permute-start | bytes 63944 | tf_op jit(solution)/shard_map/ppermute | solution.py:358
  51.6 0.8 collective-permute-done.1.other_ref
  52.5 0.0 copy-start.3
  52.5 0.0 copy-done.2
  52.5 0.6 copy-done.3
  53.1 8.7 %project.1 = (f32[48,222]{1,0:T(8,128)}, bf16[8,32,24,128]{3,2,1,0:T(8,128)(2,1)}) custom-call(s32[1]{0:T(128)} %bitcast.core_ref, f32[24,222]{1,0:T(8,128)} %copy-done.2, f32[24,222]{1,0:T(8,128)} %copy-done.3, bf16[888,4096]{1,0:T(8,128)(2,1)} %get-tuple-element.7.flat_ref), custom_call_target="tpu_custom_call" | custom-call | tf_op jit(solution)/shard_map/project/pallas_call | solution.py:254
  61.7 0.0 copy-start.1
  61.7 46.7 %all_to_all.32.got_ref = bf16[256,24,128]{2,1,0:T(8,128)(2,1)S(1)} all-to-all(bf16[256,24,128]{2,1,0:T(8,128)(2,1)} %bitcast.16), channel_id=1, replica_groups=mesh['zl'=2,'co'=2,'y'=4,'zh'=4,'x'=4] {'zl','co','y','zh','x'}, dimensions={0} | all-to-all | bytes 3145728 | tf_op jit(solution)/shard_map/all_to_all | solution.py:362
  108.5 0.0 copy-done.1
  108.5 12.2 %hour_gram.1 = f32[2,16,24,512]{3,2,1,0:T(8,128)S(1)} custom-call(s32[1]{0:T(128)} %bitcast.core_ref, s32[8]{0:T(128)S(1)} %copy-done.1, bf16[256,24,128]{2,1,0:T(8,128)(2,1)S(1)} %all_to_all.32.got_ref), custom_call_target="tpu_custom_call" | custom-call | tf_op jit(solution)/shard_map/hour_gram/pallas_call | solution.py:338
  120.7 0.1 slice_bitcast_fusion
  120.8 1.2 collective-permute-start.2
  122.0 1.9 collective-permute-done.2
  123.9 0.1 fusion
  124.0 18.5 %all_to_all.33 = f32[16,24,512]{2,1,0:T(8,128)S(1)} all-to-all(f32[16,24,512]{2,1,0:T(8,128)S(1)} %fusion), channel_id=1, replica_groups=mesh['zl'=2,'co'=2,'y'=4,'zh'=4,'x'=4] {'y','x'}, dimensions={0} | all-to-all | bytes 1572864 | tf_op jit(solution)/shard_map/all_to_all | solution.py:362
  142.6 0.1 reduce_sum.38
  142.7 13.6 %all_to_all.34 = f32[8,24,512]{2,1,0:T(8,128)S(1)} all-to-all(f32[8,24,512]{2,1,0:T(8,128)S(1)} %broadcast_in_dim.14), channel_id=1, replica_groups=mesh['zl'=2,'co'=2,'y'=4,'zh'=4,'x'=4] {'zl','zh'}, dimensions={0} | all-to-all | bytes 786432 | tf_op jit(solution)/shard_map/all_to_all | solution.py:362
  156.3 0.0 copy-start
  156.3 0.1 broadcast_in_dim.15
  156.4 13.7 %all_to_all.35.mine_ref = f32[16,24,512]{2,1,0:T(8,128)S(1)} all-to-all(f32[16,24,512]{2,1,0:T(8,128)S(1)} %broadcast_in_dim.15), channel_id=1, replica_groups=mesh['zl'=2,'co'=2,'y'=4,'zh'=4,'x'=4] {'y','x'}, dimensions={0} | all-to-all | bytes 1572864 | tf_op jit(solution)/shard_map/all_to_all | solution.py:362
  170.1 5.3 %collective-permute-start.3 = (f32[16,24,512]{2,1,0:T(8,128)S(1)}, f32[16,24,512]{2,1,0:T(8,128)S(1)}, u32[]{:S(2)}, u32[]{:S(2)}) collective-permute-start(f32[16,24,512]{2,1,0:T(8,128)S(1)} %all_to_all.35.mine_ref), channel_id=1, source_target_pairs={{0,64},{64,0},{1,65},{65,1},{2,66},{66,2},{3,67},{67,3},{4,68},{68... | collective-permute-start | bytes 2359304 | tf_op jit(solution)/shard_map/ppermute | solution.py:358
  175.3 1.9 collective-permute-done.3.other_ref
  177.3 0.0 copy-done
  177.3 28.2 %truncate.1 = f32[768,768]{1,0:T(8,128)} custom-call(s32[1]{0:T(128)} %bitcast.core_ref, f32[16,24,512]{2,1,0:T(8,128)S(1)} %all_to_all.35.mine_ref, f32[16,24,512]{2,1,0:T(8,128)S(1)} %collective-permute-done.3.other_ref, f32[768,128]{1,0:T(8,128)S(1)} %copy-done), custom_call_target="tpu_custom_call" | custom-call | tf_op jit(solution)/shard_map/truncate/pallas_call | solution.py:128
  (6 shorter events, 0.2 us)
Async XLA Ops:
  14.1 4.1 %collective-permute-start = (f32[24,222]{1,0:T(8,128)S(1)}, f32[24,222]{1,0:T(8,128)S(1)}, u32[]{:S(2)}, u32[]{:S(2)}) collective-permute-start(f32[24,222]{1,0:T(8,128)S(1)} %slice_bitcast_fusion.2), channel_id=1, source_target_pairs={{0,64},{64,0},{1,65},{65,1},{2,66},{66,2},{3,67},{67,3},{4,68},{68... | collective-permute-start | bytes 63944 | tf_op jit(solution)/shard_map/ppermute | solution.py:358
  48.8 3.6 %copy-start.2 = (f32[24,222]{1,0:T(8,128)}, f32[24,222]{1,0:T(8,128)S(1)}, u32[]{:S(2)}) copy-start(f32[24,222]{1,0:T(8,128)S(1)} %reduce_sum.37.mine_ref) | copy-start | bytes 63940
  48.9 3.6 %collective-permute-start.1 = (f32[24,222]{1,0:T(8,128)S(1)}, f32[24,222]{1,0:T(8,128)S(1)}, u32[]{:S(2)}, u32[]{:S(2)}) collective-permute-start(f32[24,222]{1,0:T(8,128)S(1)} %reduce_sum.37.mine_ref), channel_id=1, source_target_pairs={{0,64},{64,0},{1,65},{65,1},{2,66},{66,2},{3,67},{67,3},{4,68},{68... | collective-permute-start | bytes 63944 | tf_op jit(solution)/shard_map/ppermute | solution.py:358
  52.5 0.6 copy-start.3
  61.7 46.8 %copy-start.1 = (s32[8]{0:T(128)S(1)}, s32[8]{0:T(128)}, u32[]{:S(2)}) copy-start(s32[8]{0:T(128)} %lag_ref.1) | copy-start | bytes 100
  120.8 3.1 %collective-permute-start.2 = (f32[16,24,512]{2,1,0:T(8,128)S(1)}, f32[16,24,512]{2,1,0:T(8,128)S(1)}, u32[]{:S(2)}, u32[]{:S(2)}) collective-permute-start(f32[16,24,512]{2,1,0:T(8,128)S(1)} %slice_bitcast_fusion), channel_id=1, source_target_pairs={{0,64},{64,0},{1,65},{65,1},{2,66},{66,2},{3,67},{67,3},{4,68},{68... | collective-permute-start | bytes 2359304 | tf_op jit(solution)/shard_map/ppermute | solution.py:358
  156.3 21.0 %copy-start = (f32[768,128]{1,0:T(8,128)S(1)}, f32[768,128]{1,0:T(8,128)}, u32[]{:S(2)}) copy-start(f32[768,128]{1,0:T(8,128)} %start_ref.1) | copy-start | bytes 1179652
  170.1 7.2 %collective-permute-start.3 = (f32[16,24,512]{2,1,0:T(8,128)S(1)}, f32[16,24,512]{2,1,0:T(8,128)S(1)}, u32[]{:S(2)}, u32[]{:S(2)}) collective-permute-start(f32[16,24,512]{2,1,0:T(8,128)S(1)} %all_to_all.35.mine_ref), channel_id=1, source_target_pairs={{0,64},{64,0},{1,65},{65,1},{2,66},{66,2},{3,67},{67,3},{4,68},{68... | collective-permute-start | bytes 2359304 | tf_op jit(solution)/shard_map/ppermute | solution.py:358
where the time goes:
time: 206 us; the launch traced here: 205 us
  blocking collectives  122 us (59%)
  Pallas kernels  61.8 us (30%)
  starting transfers between devices  12.4 us (6%)
  waiting for transfers between devices  5.52 us (3%)
    all_to_all x6, blocking collectives, exchange(): return lax.all_to_all(x, axes, split_axis=0, concat_axis=0, tiled=True)  122 us
    pallas_call x1, Pallas kernels, truncate(): pl.pallas_call(truncate_kernel, out_shape=jax.ShapeDtypeStruct((width, wi...  28.2 us
    pallas_call x1, Pallas kernels, level_product(): pl.pallas_call(functools.partial(level_gram_kernel, scale), grid=(columns...  12.8 us
    ppermute x4, starting transfers between devices, other_core(): return lax.ppermute(x, 'co', [(0, 1), (1, 0)])  12.4 us
    pallas_call x1, Pallas kernels, hour_gram(): pl.pallas_call(functools.partial(hour_gram_kernel, scale), out_shape=jax....  12.2 us
    pallas_call x1, Pallas kernels, project(): pl.pallas_call(functools.partial(project_kernel, hours), grid=(columns //...  8.65 us
    ppermute x4, waiting for transfers between devices, other_core(): return lax.ppermute(x, 'co', [(0, 1), (1, 0)])  5.52 us
  transfers between devices with their start and end apart: 4, of which 4 were waited for; matrix products, arithmetic and copies ran while one was open for 0% of the time, Pallas kernels for 0%

commit v1 on v0

--- a/solution.py
+++ b/solution.py
@@ -35,42 +35,38 @@
     sub = lax.broadcasted_iota(jnp.int32, (8, LANES), 0)
     left = [gram[8 * t : 8 * t + 8, :] for t in range(tiles)]
     right = [jnp.where(lane == sub + 8 * t, 1.0, 0.0) for t in range(tiles)]
-    for i in range(0, n, 4):
-        here, off = i // 8, i % 8
+    for here in range(tiles):
         cols = [
-            {t: jnp.broadcast_to(left[t][:, i + k : i + k + 1], (8, LANES)) for t in range(here, tiles)}
-            for k in range(4)
+            {
+                t: jnp.broadcast_to(left[t][:, 8 * here + k : 8 * here + k + 1], (8, LANES))
+                for t in range(here, tiles)
+            }
+            for k in range(8)
         ]
-        entry = lambda r, k: across(cols[k][here][off + r : off + r + 1, :])
+        entry = {(r, k): across(cols[k][here][r : r + 1, :]) for k in range(8) for r in range(k, 8)}
         low, inv = {}, []
-        for k in range(4):
-            for r in range(k, 4):
-                v = entry(r, k)
-                for q in range(k):
-                    v = v - low[r, q] * low[k, q]
-                if r == k:
-                    inv.append(lax.rsqrt(v))
-                else:
-                    low[r, k] = v * inv[k]
-        rows = []
-        for k in range(4):
-            a = across(left[here][off + k : off + k + 1, :])
-            b = across(right[here][off + k : off + k + 1, :])
-            for q in range(k):
-                a = a - low[k, q] * rows[q][0]
-                b = b - low[k, q] * rows[q][1]
-            rows.append((a * inv[k], b * inv[k]))
-            out_ref[i + k : i + k + 1, :] = rows[k][1][0:1, :]
-        for t in range(here + (off > 0), tiles):
-            mult = []
-            for k in range(4):
-                v = cols[k][t]
-                for q in range(k):
-                    v = v - mult[q] * low[k, q]
-                mult.append(v * inv[k])
-            for k in range(4):
-                left[t] = left[t] - mult[k] * rows[k][0]
-                right[t] = right[t] - mult[k] * rows[k][1]
+        for k in range(8):
+            inv.append(lax.rsqrt(entry[k, k]))
+            for r in range(k + 1, 8):
+                low[r, k] = entry[r, k] * inv[k]
+            for q in range(k + 1, 8):
+                for r in range(q, 8):
+                    entry[r, q] = entry[r, q] - low[r, k] * low[q, k]
+        side = [across(left[here][k : k + 1, :]) for k in range(8)], [across(right[here][k : k + 1, :]) for k in range(8)]
+        for k in range(8):
+            for row in side:
+                row[k] = row[k] * inv[k]
+                for r in range(k + 1, 8):
+                    row[r] = row[r] - low[r, k] * row[k]
+            out_ref[8 * here + k : 8 * here + k + 1, :] = side[1][k][0:1, :]
+        for t in range(here + 1, tiles):
+            mult = [cols[k][t] for k in range(8)]
+            for k in range(8):
+                mult[k] = mult[k] * inv[k]
+                for r in range(k + 1, 8):
+                    mult[r] = mult[r] - mult[k] * low[r, k]
+                left[t] = left[t] - mult[k] * side[0][k]
+                right[t] = right[t] - mult[k] * side[1][k]
 
 
 def truncate_kernel(core_ref, mine_ref, other_ref, start_ref, out_ref, d_ref, half_ref, split_ref, z_ref, w_ref, linv_ref):
@@ -118,7 +114,7 @@
     linv = linv_ref[...]
     basis = dot(linv, z_ref[...])
     inner = dot(dot(linv, w_ref[...]), basis, ((1,), (1,)))
-    out_ref[...] = dot(basis, dot(inner, basis), ((0,), (0,)))
+    out_ref[...] = dot(basis, dot(inner, basis), ((0,), (0,)), lax.Precision.HIGH)
 
 
 def truncate(core, mine, other, start):
@@ -147,11 +143,11 @@
     return lax.broadcasted_iota(jnp.int32, shape, axis)
 
 
-def spread(levels, hours, turned=False):
+def spread(levels, hours, places, turned=False):
     if turned:
-        place, level = counted((levels * hours, 1), 0), counted((1, levels), 1)
+        place, level = counted((places, 1), 0), counted((1, levels), 1)
     else:
-        place, level = counted((1, levels * hours), 1), counted((levels, 1), 0)
+        place, level = counted((1, places), 1), counted((levels, 1), 0)
     first = level * hours
     return jnp.where((place >= first) & (place < first + hours), 1.0, 0.0).astype(jnp.bfloat16)
 
@@ -160,118 +156,124 @@
     return of(counted((rows, 1), 0)) == of(counted((1, columns), 1))
 
 
-def level_gram_kernel(scale, core_ref, field_ref, start_ref, out_ref, flat_ref, acc_ref):
-    step = pl.program_id(0)
-    levels, hours, chunk = field_ref.shape
-    total = levels * hours
+def level_gram_kernel(scale, core_ref, field_ref, start_ref, out_ref, flat_ref, acc_ref, field_vmem, flat_vmem, sems, flat_sems):
+    levels, hours, columns = field_ref.shape
+    total = flat_ref.shape[0]
+    chunk = columns // sems.shape[0]
     tile = 256
-
-    @pl.when(step == 0)
-    def _():
-        acc_ref[...] = jnp.zeros_like(acc_ref)
-
-    flat = field_ref[...].reshape(total, chunk)
-    flat_ref[...] = flat
-    for j in range(0, total, tile):
-        wide = min(tile, total - j)
-        acc_ref[j:, j : j + wide] += dot(flat[j:], flat[j : j + wide], ((1,), (1,)), None)
-
-    @pl.when(step == pl.num_programs(0) - 1)
-    def _():
-        weight = jnp.where(same(total, total, lambda i: lax.div(i, tile)), 0.5, 1.0)
-        weight = jnp.where(same(total, total, lambda i: lax.rem(i, hours)), weight, 0.0)
-        half = acc_ref[...] * weight
-        left = spread(levels, hours)
-        right = spread(levels, hours, True)
-        over = sum(dot(left, part, precision=None) for part in reversed(split(half)))
-        gram = sum(dot(part, right, precision=None) for part in reversed(split(over)))
-        z = (dot(start_ref[...], gram) + dot(start_ref[...], gram, ((1,), (1,)))) * scale
-        part = out_ref.shape[1]
-        for c in range(2):
-            out_ref[lax.bitwise_xor(c, core_ref[0])] = z[part * c : part * (c + 1)]
+    copies, writes = [], []
+    for c in range(sems.shape[0]):
+        at = pl.ds(c * chunk, chunk)
+        copies.append(pltpu.make_async_copy(field_ref.at[:, :, at], field_vmem.at[:, :, at], sems.at[c]))
+        copies[c].start()
+    for c, copy in enumerate(copies):
+        copy.wait()
+        flat = field_vmem[:, :, c * chunk : (c + 1) * chunk].reshape(levels * hours, chunk)
+        flat = jnp.concatenate([flat, jnp.zeros((total - levels * hours, chunk), jnp.bfloat16)], axis=0)
+        at = pl.ds(c * chunk, chunk)
+        flat_vmem[:, at] = flat
+        writes.append(pltpu.make_async_copy(flat_vmem.at[:, at], flat_ref.at[:, at], flat_sems.at[c]))
+        writes[c].start()
+        for j in range(0, total, tile):
+            wide = min(tile, total - j)
+            block = dot(flat[j:], flat[j : j + wide], ((1,), (1,)), None)
+            acc_ref[j:, j : j + wide] = block if c == 0 else acc_ref[j:, j : j + wide] + block
+    for j in range(tile, total, tile):
+        acc_ref[j - tile : j, j:] = jnp.zeros((tile, total - j), jnp.float32)
+    weight = jnp.where(same(total, total, lambda i: lax.div(i, tile)), 0.5, 1.0)
+    weight = jnp.where(same(total, total, lambda i: lax.rem(i, hours)), weight, 0.0)
+    half = acc_ref[...] * weight
+    left = spread(levels, hours, total)
+    right = spread(levels, hours, total, True)
+    over = sum(dot(left, part, precision=None) for part in reversed(split(half)))
+    gram = sum(dot(part, right, precision=None) for part in reversed(split(over)))
+    z = (dot(start_ref[...], gram) + dot(start_ref[...], gram, ((1,), (1,)))) * scale
+    part = out_ref.shape[1]
+    for c in range(2):
+        out_ref[lax.bitwise_xor(c, core_ref[0])] = z[part * c : part * (c + 1)]
+    for write in writes:
+        write.wait()
 
 
 def level_product(core, field, start, scale):
     levels, hours, columns = field.shape
     nmodes = start.shape[0]
-    chunk = 1024
+    total = -(-levels * hours // 16) * 16
+    smem, vm = pl.BlockSpec(memory_space=pltpu.SMEM), pl.BlockSpec(memory_space=pltpu.VMEM)
     return pl.pallas_call(
         functools.partial(level_gram_kernel, scale),
-        grid=(columns // chunk,),
         out_shape=(
             jax.ShapeDtypeStruct((2, nmodes // 2, levels), jnp.float32),
-            jax.ShapeDtypeStruct((levels * hours, columns), jnp.bfloat16),
+            jax.ShapeDtypeStruct((total, columns), jnp.bfloat16),
         ),
-        in_specs=[
-            pl.BlockSpec(memory_space=pltpu.SMEM),
-            pl.BlockSpec((levels, hours, chunk), lambda c: (0, 0, c)),
-            pl.BlockSpec((nmodes, levels), lambda c: (0, 0)),
+        in_specs=[smem, pl.BlockSpec(memory_space=pltpu.HBM), vm],
+        out_specs=(vm, pl.BlockSpec(memory_space=pltpu.HBM)),
+        scratch_shapes=[
+            pltpu.VMEM((total, total), jnp.float32),
+            pltpu.VMEM((levels, hours, columns), jnp.bfloat16),
+            pltpu.VMEM((total, columns), jnp.bfloat16),
+            pltpu.SemaphoreType.DMA((4,)),
+            pltpu.SemaphoreType.DMA((4,)),
         ],
-        out_specs=(
-            pl.BlockSpec((2, nmodes // 2, levels), lambda c: (0, 0, 0)),
-            pl.BlockSpec((levels * hours, chunk), lambda c: (0, c)),
-        ),
-        scratch_shapes=[pltpu.VMEM((levels * hours, levels * hours), jnp.float32)],
         compiler_params=pltpu.CompilerParams(vmem_limit_bytes=60 * 2**20),
         name="level_product",
     )(core, field, start)
 
 
-def project_kernel(hours, core_ref, mine_ref, other_ref, flat_ref, basis_ref, out_ref, weight_ref, linv_ref, z_ref):
-    total, chunk = flat_ref.shape
+def project_kernel(hours, core_ref, mine_ref, other_ref, flat_ref, basis_ref, out_ref, weight_ref, linv_ref, z_ref, flat_vmem, sems):
+    total, columns = flat_ref.shape
+    chunk = columns // sems.shape[0]
+    copies = []
+    for c in range(sems.shape[0]):
+        at = pl.ds(c * chunk, chunk)
+        copies.append(pltpu.make_async_copy(flat_ref.at[:, at], flat_vmem.at[:, at], sems.at[c]))
+        copies[c].start()
     nmodes, levels = z_ref.shape
     f32, bf16 = jnp.float32, jnp.bfloat16
 
-    @pl.when(pl.program_id(0) == 0)
-    def _():
-        part = nmodes // 2
-        z_ref[pl.ds(pl.multiple_of(part * core_ref[0], 8), part), :] = mine_ref[...]
-        z_ref[pl.ds(pl.multiple_of(part * (1 - core_ref[0]), 8), part), :] = other_ref[...]
-        z = z_ref[...]
-        gram = dot(z, z, ((1,), (1,)))
-        padded = jnp.concatenate([gram, jnp.zeros((nmodes, LANES - nmodes), f32)], axis=1)
-        inverse_cholesky(padded, linv_ref)
-        basis = dot(linv_ref[:, :nmodes], z)
-        basis_ref[...] = basis
-        modes_by_hours = spread(nmodes, hours, True)
-        tall = dot(modes_by_hours, basis.astype(bf16), precision=None).astype(bf16)
-        wide = dot(tall, spread(levels, hours), precision=None)
-        weight_ref[...] = jnp.where(same(*wide.shape, lambda i: lax.rem(i, hours)), wide, 0.0).astype(bf16)
-
-    made = dot(weight_ref[...], flat_ref[...], precision=None)
-    groups, blocks, rows, _ = out_ref.shape
-    for a in range(groups):
-        for b in range(blocks):
-            out_ref[a, b] = made[rows * a : rows * (a + 1), LANES * b : LANES * (b + 1)].astype(bf16)
+    part = nmodes // 2
+    z_ref[pl.ds(pl.multiple_of(part * core_ref[0], 8), part), :] = mine_ref[...]
+    z_ref[pl.ds(pl.multiple_of(part * (1 - core_ref[0]), 8), part), :] = other_ref[...]
+    z = z_ref[...]
+    gram = dot(z, z, ((1,), (1,)))
+    padded = jnp.concatenate([gram, jnp.zeros((nmodes, LANES - nmodes), f32)], axis=1)
+    inverse_cholesky(padded, linv_ref)
+    basis = dot(linv_ref[:, :nmodes], z)
+    basis_ref[...] = basis
+    modes_by_hours = spread(nmodes, hours, nmodes * hours, True)
+    tall = dot(modes_by_hours, basis.astype(bf16), precision=None).astype(bf16)
+    wide = dot(tall, spread(levels, hours, total), precision=None)
+    weight_ref[...] = jnp.where(same(*wide.shape, lambda i: lax.rem(i, hours)), wide, 0.0).astype(bf16)
+
+    groups, _, rows, _ = out_ref.shape
+    for c, copy in enumerate(copies):
+        copy.wait()
+        made = dot(weight_ref[...], flat_vmem[:, c * chunk : (c + 1) * chunk], precision=None)
+        for a in range(groups):
+            for b in range(chunk // LANES):
+                out_ref[a, c * chunk // LANES + b] = made[rows * a : rows * (a + 1), LANES * b : LANES * (b + 1)].astype(bf16)
 
 
 def project(core, mine, other, flat, hours, groups):
     total, columns = flat.shape
     part, levels = mine.shape
     nmodes = 2 * part
-    chunk = 1024
     rows = hours * nmodes // groups
+    smem, vm = pl.BlockSpec(memory_space=pltpu.SMEM), pl.BlockSpec(memory_space=pltpu.VMEM)
     return pl.pallas_call(
         functools.partial(project_kernel, hours),
-        grid=(columns // chunk,),
         out_shape=(
             jax.ShapeDtypeStruct((nmodes, levels), jnp.float32),
             jax.ShapeDtypeStruct((groups, columns // LANES, rows, LANES), jnp.bfloat16),
         ),
-        in_specs=[
-            pl.BlockSpec(memory_space=pltpu.SMEM),
-            pl.BlockSpec((part, levels), lambda c: (0, 0)),
-            pl.BlockSpec((part, levels), lambda c: (0, 0)),
-            pl.BlockSpec((total, chunk), lambda c: (0, c)),
-        ],
-        out_specs=(
-            pl.BlockSpec((nmodes, levels), lambda c: (0, 0)),
-            pl.BlockSpec((groups, chunk // LANES, rows, LANES), lambda c: (0, c, 0, 0)),
-        ),
+        in_specs=[smem, vm, vm, pl.BlockSpec(memory_space=pltpu.HBM)],
+        out_specs=(vm, vm),
         scratch_shapes=[
             pltpu.VMEM((hours * nmodes, total), jnp.bfloat16),
             pltpu.VMEM((nmodes, LANES), jnp.float32),
             pltpu.VMEM((nmodes, levels), jnp.float32),
+            pltpu.VMEM((total, columns), jnp.bfloat16),
+            pltpu.SemaphoreType.DMA((4,)),
         ],
         compiler_params=pltpu.CompilerParams(vmem_limit_bytes=60 * 2**20),
         name="project",
@@ -304,25 +306,23 @@
         for b in range(gram_ref.shape[0]):
             gram_ref[b, i : i + 256, :] = band[:, LANES * b : LANES * (b + 1)]
 
-    blocks = width // LANES
-    lane = lax.broadcasted_iota(jnp.int32, (LANES, LANES), 1)
+    blocks, some = width // LANES, 32
+    lane = lax.broadcasted_iota(jnp.int32, (some, LANES), 1)
+    lags = [lag_ref[j] for j in range(lag_ref.shape[0])]
+    whole = [lax.div(offset, LANES) for offset in lags]
+    part = [lax.rem(offset, LANES) for offset in lags]
     for i in range(blocks):
         wanted = [(i + d) % blocks for d in range(4)]
-
-        def add(j, acc):
-            offset = lag_ref[j]
-            whole, part = lax.div(offset, LANES), lax.rem(offset, LANES)
-            turn = lax.rem(LANES - part, LANES)
-            at = offset + LANES * i
-            load = {}
-            for b in sorted(set(wanted) | {w + 1 for w in wanted}):
-                column = jnp.minimum(whole + b, gram_ref.shape[0] - 1)
-                load[b] = pltpu.roll(gram_ref[column, pl.ds(at, LANES), :], turn, 1)
-            return tuple(a + jnp.where(lane < LANES - part, load[w], load[w + 1]) for a, w in zip(acc, wanted))
-
-        acc = lax.fori_loop(0, lag_ref.shape[0], add, tuple(jnp.zeros((LANES, LANES), f32) for _ in wanted))
-        for d in range(4):
-            half_ref[LANES * i : LANES * (i + 1), LANES * d : LANES * (d + 1)] = acc[d] * scale
+        for r in range(LANES * i, LANES * (i + 1), some):
+            acc = [jnp.zeros((some, LANES), f32)] * 4
+            for j, offset in enumerate(lags):
+                load = {}
+                for b in sorted(set(wanted) | {w + 1 for w in wanted}):
+                    block = gram_ref[jnp.minimum(whole[j] + b, gram_ref.shape[0] - 1), pl.ds(offset + r, some), :]
+                    load[b] = pltpu.roll(block, lax.rem(LANES - part[j], LANES), 1)
+                acc = [a + jnp.where(lane < LANES - part[j], load[w], load[w + 1]) for a, w in zip(acc, wanted)]
+            for d in range(4):
+                half_ref[r : r + some, LANES * d : LANES * (d + 1)] = acc[d] * scale
     _, each, high, _ = out_ref.shape
     for c in range(2):
         for k in range(each):

time: 206 us -> 195 us (0.947)
  Pallas kernels: 61.8 us -> 50.8 us
    pallas_call x1, Pallas kernels: 12.2 us -> 8.23 us  [hour_gram(): pl.pallas_call(functools.partial(hour_gram_kernel, scale), out_shape=jax....]
    pallas_call x1, Pallas kernels: 28.2 us -> 24.2 us  [truncate(): pl.pallas_call(truncate_kernel, out_shape=jax.ShapeDtypeStruct((width, wi...]
    pallas_call x2, Pallas kernels: 21.4 us -> 18.4 us  [the longest x1 11.1 us: level_product(): pl.pallas_call(functools.partial(level_gram_kernel, scale), out_shape=(ja...]
where the time goes in v1:
time: 195 us; the launch traced here: 194 us
  blocking collectives  122 us (63%)
  Pallas kernels  50.8 us (26%)
  starting transfers between devices  12.4 us (6%)
  waiting for transfers between devices  5.52 us (3%)
    all_to_all x6, blocking collectives, exchange(): return lax.all_to_all(x, axes, split_axis=0, concat_axis=0, tiled=True)  122 us
    pallas_call x1, Pallas kernels, truncate(): pl.pallas_call(truncate_kernel, out_shape=jax.ShapeDtypeStruct((width, wi...  24.2 us
    ppermute x4, starting transfers between devices, other_core(): return lax.ppermute(x, 'co', [(0, 1), (1, 0)])  12.4 us
    pallas_call x1, Pallas kernels, level_product(): pl.pallas_call(functools.partial(level_gram_kernel, scale), out_shape=(ja...  11.1 us
    pallas_call x1, Pallas kernels, hour_gram(): pl.pallas_call(functools.partial(hour_gram_kernel, scale), out_shape=jax....  8.23 us
    pallas_call x1, Pallas kernels, project(): pl.pallas_call(functools.partial(project_kernel, hours), out_shape=(jax.S...  7.27 us
    ppermute x4, waiting for transfers between devices, other_core(): return lax.ppermute(x, 'co', [(0, 1), (1, 0)])  5.52 us
  transfers between devices with their start and end apart: 4, of which 4 were waited for; matrix products, arithmetic and copies ran while one was open for 0% of the time, Pallas kernels for 0%

profile of v1, /device:TPU:1, one launch (start us, length us, event | category | flops | bytes accessed | tf_op | source)
XLA Modules:
  0.0 194.5 jit_solution(4539629538668247843)
XLA Ops:
  0.6 11.1 %level_product.1 = (f32[2,24,222]{2,1,0:T(8,128)}, bf16[896,4096]{1,0:T(8,128)(2,1)}) custom-call(s32[1]{0:T(128)} %bitcast.core_ref, bf16[222,4,4096]{2,1,0:T(4,128)(2,1)} %bitcast.15, f32[48,222]{1,0:T(8,128)} %bitcast.17), custom_call_target="tpu_custom_call" | custom-call | tf_op jit(solution)/shard_map/level_product/pallas_call | solution.py:203
  11.7 0.7 slice_bitcast_fusion.2
  12.5 3.2 %collective-permute-start = (f32[24,222]{1,0:T(8,128)S(1)}, f32[24,222]{1,0:T(8,128)S(1)}, u32[]{:S(2)}, u32[]{:S(2)}) collective-permute-start(f32[24,222]{1,0:T(8,128)S(1)} %slice_bitcast_fusion.2), channel_id=1, source_target_pairs={{0,64},{64,0},{1,65},{65,1},{2,66},{66,2},{3,67},{67,3},{4,68},{68... | collective-permute-start | bytes 63944 | tf_op jit(solution)/shard_map/ppermute | solution.py:358
  15.7 0.8 collective-permute-done
  16.6 0.7 bitcast_add_fusion
  17.3 14.4 %all_to_all.30 = f32[16,24,222]{2,1,0:T(8,128)S(1)} all-to-all(f32[16,24,222]{2,1,0:T(8,128)S(1)} %broadcast_in_dim.12), channel_id=1, replica_groups=mesh['zl'=2,'co'=2,'y'=4,'zh'=4,'x'=4] {'y','x'}, dimensions={0} | all-to-all | bytes 681984 | tf_op jit(solution)/shard_map/all_to_all | solution.py:362
  31.8 15.4 %all_to_all.31 = f32[8,24,222]{2,1,0:T(8,128)S(1)} all-to-all(f32[8,24,222]{2,1,0:T(8,128)S(1)} %broadcast_in_dim.13), channel_id=1, replica_groups=mesh['zl'=2,'co'=2,'y'=4,'zh'=4,'x'=4] {'zl','zh'}, dimensions={0} | all-to-all | bytes 340992 | tf_op jit(solution)/shard_map/all_to_all | solution.py:362
  47.2 0.0 copy-start.2
  47.2 2.8 %collective-permute-start.1 = (f32[24,222]{1,0:T(8,128)S(1)}, f32[24,222]{1,0:T(8,128)S(1)}, u32[]{:S(2)}, u32[]{:S(2)}) collective-permute-start(f32[24,222]{1,0:T(8,128)S(1)} %reduce_sum.37.mine_ref), channel_id=1, source_target_pairs={{0,64},{64,0},{1,65},{65,1},{2,66},{66,2},{3,67},{67,3},{4,68},{68... | collective-permute-start | bytes 63944 | tf_op jit(solution)/shard_map/ppermute | solution.py:358
  49.9 0.8 collective-permute-done.1.other_ref
  50.8 0.0 copy-start.3
  50.8 0.0 copy-done.2
  50.8 0.6 copy-done.3
  51.4 7.3 %project.1 = (f32[48,222]{1,0:T(8,128)}, bf16[8,32,24,128]{3,2,1,0:T(8,128)(2,1)}) custom-call(s32[1]{0:T(128)} %bitcast.core_ref, f32[24,222]{1,0:T(8,128)} %copy-done.2, f32[24,222]{1,0:T(8,128)} %copy-done.3, bf16[896,4096]{1,0:T(8,128)(2,1)} %get-tuple-element.7.flat_ref), custom_call_target="tpu_custom_call" | custom-call | tf_op jit(solution)/shard_map/project/pallas_call | solution.py:263
  58.7 0.0 copy-start.1
  58.7 46.8 %all_to_all.32.got_ref = bf16[256,24,128]{2,1,0:T(8,128)(2,1)S(1)} all-to-all(bf16[256,24,128]{2,1,0:T(8,128)(2,1)} %bitcast.16), channel_id=1, replica_groups=mesh['zl'=2,'co'=2,'y'=4,'zh'=4,'x'=4] {'zl','co','y','zh','x'}, dimensions={0} | all-to-all | bytes 3145728 | tf_op jit(solution)/shard_map/all_to_all | solution.py:362
  105.5 0.0 copy-done.1
  105.5 8.2 %hour_gram.1 = f32[2,16,24,512]{3,2,1,0:T(8,128)S(1)} custom-call(s32[1]{0:T(128)} %bitcast.core_ref, s32[8]{0:T(128)S(1)} %copy-done.1, bf16[256,24,128]{2,1,0:T(8,128)(2,1)S(1)} %all_to_all.32.got_ref), custom_call_target="tpu_custom_call" | custom-call | tf_op jit(solution)/shard_map/hour_gram/pallas_call | solution.py:338
  113.7 0.1 slice_bitcast_fusion
  113.8 1.2 collective-permute-start.2
  115.0 1.9 collective-permute-done.2
  116.9 0.1 fusion
  117.0 18.5 %all_to_all.33 = f32[16,24,512]{2,1,0:T(8,128)S(1)} all-to-all(f32[16,24,512]{2,1,0:T(8,128)S(1)} %fusion), channel_id=1, replica_groups=mesh['zl'=2,'co'=2,'y'=4,'zh'=4,'x'=4] {'y','x'}, dimensions={0} | all-to-all | bytes 1572864 | tf_op jit(solution)/shard_map/all_to_all | solution.py:362
  135.6 0.1 reduce_sum.38
  135.7 13.6 %all_to_all.34 = f32[8,24,512]{2,1,0:T(8,128)S(1)} all-to-all(f32[8,24,512]{2,1,0:T(8,128)S(1)} %broadcast_in_dim.14), channel_id=1, replica_groups=mesh['zl'=2,'co'=2,'y'=4,'zh'=4,'x'=4] {'zl','zh'}, dimensions={0} | all-to-all | bytes 786432 | tf_op jit(solution)/shard_map/all_to_all | solution.py:362
  149.3 0.0 copy-start
  149.3 0.1 broadcast_in_dim.15
  149.4 13.7 %all_to_all.35.mine_ref = f32[16,24,512]{2,1,0:T(8,128)S(1)} all-to-all(f32[16,24,512]{2,1,0:T(8,128)S(1)} %broadcast_in_dim.15), channel_id=1, replica_groups=mesh['zl'=2,'co'=2,'y'=4,'zh'=4,'x'=4] {'y','x'}, dimensions={0} | all-to-all | bytes 1572864 | tf_op jit(solution)/shard_map/all_to_all | solution.py:362
  163.1 5.3 %collective-permute-start.3 = (f32[16,24,512]{2,1,0:T(8,128)S(1)}, f32[16,24,512]{2,1,0:T(8,128)S(1)}, u32[]{:S(2)}, u32[]{:S(2)}) collective-permute-start(f32[16,24,512]{2,1,0:T(8,128)S(1)} %all_to_all.35.mine_ref), channel_id=1, source_target_pairs={{0,64},{64,0},{1,65},{65,1},{2,66},{66,2},{3,67},{67,3},{4,68},{68... | collective-permute-start | bytes 2359304 | tf_op jit(solution)/shard_map/ppermute | solution.py:358
  168.3 1.9 collective-permute-done.3.other_ref
  170.3 0.0 copy-done
  170.3 24.2 %truncate.1 = f32[768,768]{1,0:T(8,128)} custom-call(s32[1]{0:T(128)} %bitcast.core_ref, f32[16,24,512]{2,1,0:T(8,128)S(1)} %all_to_all.35.mine_ref, f32[16,24,512]{2,1,0:T(8,128)S(1)} %collective-permute-done.3.other_ref, f32[768,128]{1,0:T(8,128)S(1)} %copy-done), custom_call_target="tpu_custom_call" | custom-call | tf_op jit(solution)/shard_map/truncate/pallas_call | solution.py:124
  (6 shorter events, 0.2 us)
Async XLA Ops:
  12.5 4.1 %collective-permute-start = (f32[24,222]{1,0:T(8,128)S(1)}, f32[24,222]{1,0:T(8,128)S(1)}, u32[]{:S(2)}, u32[]{:S(2)}) collective-permute-start(f32[24,222]{1,0:T(8,128)S(1)} %slice_bitcast_fusion.2), channel_id=1, source_target_pairs={{0,64},{64,0},{1,65},{65,1},{2,66},{66,2},{3,67},{67,3},{4,68},{68... | collective-permute-start | bytes 63944 | tf_op jit(solution)/shard_map/ppermute | solution.py:358
  47.2 3.6 %copy-start.2 = (f32[24,222]{1,0:T(8,128)}, f32[24,222]{1,0:T(8,128)S(1)}, u32[]{:S(2)}) copy-start(f32[24,222]{1,0:T(8,128)S(1)} %reduce_sum.37.mine_ref) | copy-start | bytes 63940
  47.2 3.6 %collective-permute-start.1 = (f32[24,222]{1,0:T(8,128)S(1)}, f32[24,222]{1,0:T(8,128)S(1)}, u32[]{:S(2)}, u32[]{:S(2)}) collective-permute-start(f32[24,222]{1,0:T(8,128)S(1)} %reduce_sum.37.mine_ref), channel_id=1, source_target_pairs={{0,64},{64,0},{1,65},{65,1},{2,66},{66,2},{3,67},{67,3},{4,68},{68... | collective-permute-start | bytes 63944 | tf_op jit(solution)/shard_map/ppermute | solution.py:358
  50.8 0.6 copy-start.3
  58.7 46.8 %copy-start.1 = (s32[8]{0:T(128)S(1)}, s32[8]{0:T(128)}, u32[]{:S(2)}) copy-start(s32[8]{0:T(128)} %lag_ref.1) | copy-start | bytes 100
  113.8 3.1 %collective-permute-start.2 = (f32[16,24,512]{2,1,0:T(8,128)S(1)}, f32[16,24,512]{2,1,0:T(8,128)S(1)}, u32[]{:S(2)}, u32[]{:S(2)}) collective-permute-start(f32[16,24,512]{2,1,0:T(8,128)S(1)} %slice_bitcast_fusion), channel_id=1, source_target_pairs={{0,64},{64,0},{1,65},{65,1},{2,66},{66,2},{3,67},{67,3},{4,68},{68... | collective-permute-start | bytes 2359304 | tf_op jit(solution)/shard_map/ppermute | solution.py:358
  149.3 21.0 %copy-start = (f32[768,128]{1,0:T(8,128)S(1)}, f32[768,128]{1,0:T(8,128)}, u32[]{:S(2)}) copy-start(f32[768,128]{1,0:T(8,128)} %start_ref.1) | copy-start | bytes 1179652
  163.1 7.2 %collective-permute-start.3 = (f32[16,24,512]{2,1,0:T(8,128)S(1)}, f32[16,24,512]{2,1,0:T(8,128)S(1)}, u32[]{:S(2)}, u32[]{:S(2)}) collective-permute-start(f32[16,24,512]{2,1,0:T(8,128)S(1)} %all_to_all.35.mine_ref), channel_id=1, source_target_pairs={{0,64},{64,0},{1,65},{65,1},{2,66},{66,2},{3,67},{67,3},{4,68},{68... | collective-permute-start | bytes 2359304 | tf_op jit(solution)/shard_map/ppermute | solution.py:358

commit v2 on v1

--- a/solution.py
+++ b/solution.py
@@ -69,20 +69,17 @@
                 right[t] = right[t] - mult[k] * side[1][k]
 
 
-def truncate_kernel(core_ref, mine_ref, other_ref, start_ref, out_ref, d_ref, half_ref, split_ref, z_ref, w_ref, linv_ref):
+def truncate_kernel(core_ref, mine_ref, other_ref, start_ref, out_ref, d_ref, half_ref, split_ref, z_ref, w_ref, linv_ref, sems):
     each, high, _ = mine_ref.shape
     width = d_ref.shape[0]
     for ref, core in ((mine_ref, core_ref[0]), (other_ref, 1 - core_ref[0])):
         for k in range(each):
             half_ref[pl.ds(pl.multiple_of((core * each + k) * high, 8), high), :] = ref[k]
-    blocks = width // LANES
-    for i in range(blocks):
-        for d in range(4):
-            j = (i + d) % blocks
-            block = half_ref[LANES * i : LANES * (i + 1), LANES * d : LANES * (d + 1)]
-            d_ref[LANES * i : LANES * (i + 1), LANES * j : LANES * (j + 1)] = block
-            if d in (1, 2):
-                d_ref[LANES * j : LANES * (j + 1), LANES * i : LANES * (i + 1)] = block.T
+    for (down, along), (i, j) in stored(width // LANES):
+        block = half_ref[LANES * down : LANES * (down + 1), LANES * along : LANES * (along + 1)]
+        d_ref[LANES * i : LANES * (i + 1), LANES * j : LANES * (j + 1)] = block
+        if i != j:
+            d_ref[LANES * j : LANES * (j + 1), LANES * i : LANES * (i + 1)] = block.T
     lagged = d_ref[...]
     rows = jnp.sum(lagged, axis=1, keepdims=True) * (1.0 / width)
     cols = jnp.sum(lagged, axis=0, keepdims=True) * (1.0 / width)
@@ -114,7 +111,16 @@
     linv = linv_ref[...]
     basis = dot(linv, z_ref[...])
     inner = dot(dot(linv, w_ref[...]), basis, ((1,), (1,)))
-    out_ref[...] = dot(basis, dot(inner, basis), ((0,), (0,)), lax.Precision.HIGH)
+    spanned = dot(inner, basis)
+    copies = []
+    for r in range(sems.shape[0]):
+        at = pl.ds(r * width // sems.shape[0], width // sems.shape[0])
+        rows = basis[:, r * width // sems.shape[0] : (r + 1) * width // sems.shape[0]]
+        d_ref[at, :] = dot(rows, spanned, ((0,), (0,)), lax.Precision.HIGH)
+        copies.append(pltpu.make_async_copy(d_ref.at[at, :], out_ref.at[at, :], sems.at[r]))
+        copies[r].start()
+    for copy in copies:
+        copy.wait()
 
 
 def truncate(core, mine, other, start):
@@ -125,7 +131,7 @@
         truncate_kernel,
         out_shape=jax.ShapeDtypeStruct((width, width), f32),
         in_specs=[pl.BlockSpec(memory_space=pltpu.SMEM), vm, vm, vm],
-        out_specs=vm,
+        out_specs=pl.BlockSpec(memory_space=pltpu.HBM),
         scratch_shapes=[
             pltpu.VMEM((width, width), f32),
             pltpu.VMEM((width, 4 * LANES), f32),
@@ -133,6 +139,7 @@
             pltpu.VMEM((rank, width), f32),
             pltpu.VMEM((rank, width), f32),
             pltpu.VMEM((rank, rank), f32),
+            pltpu.SemaphoreType.DMA((3,)),
         ],
         compiler_params=pltpu.CompilerParams(vmem_limit_bytes=48 * 2**20),
         name="truncate",
@@ -156,7 +163,7 @@
     return of(counted((rows, 1), 0)) == of(counted((1, columns), 1))
 
 
-def level_gram_kernel(scale, core_ref, field_ref, start_ref, out_ref, flat_ref, acc_ref, field_vmem, flat_vmem, sems, flat_sems):
+def level_gram_kernel(scale, core_ref, field_ref, start_ref, mine_ref, other_ref, flat_ref, acc_ref, field_vmem, flat_vmem, sems, flat_sems):
     levels, hours, columns = field_ref.shape
     total = flat_ref.shape[0]
     chunk = columns // sems.shape[0]
@@ -178,19 +185,22 @@
             wide = min(tile, total - j)
             block = dot(flat[j:], flat[j : j + wide], ((1,), (1,)), None)
             acc_ref[j:, j : j + wide] = block if c == 0 else acc_ref[j:, j : j + wide] + block
-    for j in range(tile, total, tile):
-        acc_ref[j - tile : j, j:] = jnp.zeros((tile, total - j), jnp.float32)
-    weight = jnp.where(same(total, total, lambda i: lax.div(i, tile)), 0.5, 1.0)
-    weight = jnp.where(same(total, total, lambda i: lax.rem(i, hours)), weight, 0.0)
-    half = acc_ref[...] * weight
     left = spread(levels, hours, total)
     right = spread(levels, hours, total, True)
-    over = sum(dot(left, part, precision=None) for part in reversed(split(half)))
+    over = []
+    for j in range(0, total, tile):
+        wide = min(tile, total - j)
+        row, col = counted((total - j, 1), 0), counted((1, wide), 1)
+        weight = jnp.where(lax.rem(row, hours) == lax.rem(col, hours), jnp.where(row < wide, 0.5, 1.0), 0.0)
+        half = acc_ref[j:, j : j + wide] * weight
+        over.append(sum(dot(left[:, j:], part, precision=None) for part in reversed(split(half))))
+    over = jnp.concatenate(over, axis=1)
     gram = sum(dot(part, right, precision=None) for part in reversed(split(over)))
     z = (dot(start_ref[...], gram) + dot(start_ref[...], gram, ((1,), (1,)))) * scale
-    part = out_ref.shape[1]
-    for c in range(2):
-        out_ref[lax.bitwise_xor(c, core_ref[0])] = z[part * c : part * (c + 1)]
+    part = z.shape[0] // 2
+    first = core_ref[0] == 0
+    mine_ref[...] = jnp.where(first, z[:part], z[part:])
+    other_ref[...] = jnp.where(first, z[part:], z[:part])
     for write in writes:
         write.wait()
 
@@ -203,11 +213,12 @@
     return pl.pallas_call(
         functools.partial(level_gram_kernel, scale),
         out_shape=(
-            jax.ShapeDtypeStruct((2, nmodes // 2, levels), jnp.float32),
+            jax.ShapeDtypeStruct((nmodes // 2, levels), jnp.float32),
+            jax.ShapeDtypeStruct((nmodes // 2, levels), jnp.float32),
             jax.ShapeDtypeStruct((total, columns), jnp.bfloat16),
         ),
         in_specs=[smem, pl.BlockSpec(memory_space=pltpu.HBM), vm],
-        out_specs=(vm, pl.BlockSpec(memory_space=pltpu.HBM)),
+        out_specs=(vm, vm, pl.BlockSpec(memory_space=pltpu.HBM)),
         scratch_shapes=[
             pltpu.VMEM((total, total), jnp.float32),
             pltpu.VMEM((levels, hours, columns), jnp.bfloat16),
@@ -215,7 +226,7 @@
             pltpu.SemaphoreType.DMA((4,)),
             pltpu.SemaphoreType.DMA((4,)),
         ],
-        compiler_params=pltpu.CompilerParams(vmem_limit_bytes=60 * 2**20),
+        compiler_params=pltpu.CompilerParams(vmem_limit_bytes=58 * 2**20),
         name="level_product",
     )(core, field, start)
 
@@ -275,9 +286,14 @@
             pltpu.VMEM((total, columns), jnp.bfloat16),
             pltpu.SemaphoreType.DMA((4,)),
         ],
-        compiler_params=pltpu.CompilerParams(vmem_limit_bytes=60 * 2**20),
+        compiler_params=pltpu.CompilerParams(vmem_limit_bytes=58 * 2**20),
         name="project",
     )(core, mine, other, flat)
+
+
+def stored(blocks):
+    pairs = [((i, j - i), (i, j)) for i in range(blocks) for j in range(i, min(i + 4, blocks))]
+    return pairs + [((3, 3), (0, 4)), ((4, 2), (0, 5)), ((4, 3), (1, 5))]
 
 
 def hour_gram_kernel(scale, core_ref, lag_ref, got_ref, out_ref, flat_ref, gram_ref, half_ref):
@@ -302,27 +318,31 @@
                     span * m : span * (m + 1), LANES * k : LANES * (k + 1)
                 ]
     for i in range(0, flat_ref.shape[0], 256):
-        band = dot(flat_ref[i : i + 256, :], flat_ref[...], ((1,), (1,)), None)
-        for b in range(gram_ref.shape[0]):
-            gram_ref[b, i : i + 256, :] = band[:, LANES * b : LANES * (b + 1)]
+        first = max(i - LANES, 0)
+        band = dot(flat_ref[i : i + 256, :], flat_ref[first:, :], ((1,), (1,)), None)
+        for b in range(first // LANES, gram_ref.shape[0]):
+            gram_ref[b, i : i + 256, :] = band[:, LANES * b - first : LANES * (b + 1) - first]
 
     blocks, some = width // LANES, 32
     lane = lax.broadcasted_iota(jnp.int32, (some, LANES), 1)
     lags = [lag_ref[j] for j in range(lag_ref.shape[0])]
     whole = [lax.div(offset, LANES) for offset in lags]
     part = [lax.rem(offset, LANES) for offset in lags]
+    spots = {pair: spot for spot, pair in stored(blocks)}
     for i in range(blocks):
-        wanted = [(i + d) % blocks for d in range(4)]
-        for r in range(LANES * i, LANES * (i + 1), some):
-            acc = [jnp.zeros((some, LANES), f32)] * 4
+        for r in range(0, LANES, some):
+            acc = {b: jnp.zeros((some, LANES), f32) for b in range(i, blocks)}
             for j, offset in enumerate(lags):
                 load = {}
-                for b in sorted(set(wanted) | {w + 1 for w in wanted}):
-                    block = gram_ref[jnp.minimum(whole[j] + b, gram_ref.shape[0] - 1), pl.ds(offset + r, some), :]
+                for b in range(i, blocks + 1):
+                    column = jnp.minimum(whole[j] + b, gram_ref.shape[0] - 1)
+                    block = gram_ref[column, pl.ds(offset + LANES * i + r, some), :]
                     load[b] = pltpu.roll(block, lax.rem(LANES - part[j], LANES), 1)
-                acc = [a + jnp.where(lane < LANES - part[j], load[w], load[w + 1]) for a, w in zip(acc, wanted)]
-            for d in range(4):
-                half_ref[r : r + some, LANES * d : LANES * (d + 1)] = acc[d] * scale
+                acc = {b: acc[b] + jnp.where(lane < LANES - part[j], load[b], load[b + 1]) for b in acc}
+            for b in acc:
+                down, along = spots[i, b]
+                half_ref[LANES * down + r : LANES * down + r + some, LANES * along : LANES * (along + 1)] = acc[b] * scale
+    half_ref[width - LANES :, LANES:] = jnp.zeros((LANES, half_ref.shape[1] - LANES), f32)
     _, each, high, _ = out_ref.shape
     for c in range(2):
         for k in range(each):
@@ -384,8 +404,8 @@
     nmodes = level_start.shape[1]
     core = lax.axis_index("co").reshape(1)
     scale = 1.0 / (hours_all * columns)
-    halves, level_hours = level_product(core, jnp.transpose(field, (1, 0, 2)), level_start.T, scale)
-    z = halves[0] + other_core(halves[1])
+    z, other, level_hours = level_product(core, jnp.transpose(field, (1, 0, 2)), level_start.T, scale)
+    z = z + other_core(other)
     z = sum_over(sum_over(z, PLANE), COLUMN)
     level_basis, sent = project(core, z, other_core(z), level_hours, hour_count, 8)
     sent = sent.reshape(devices, 24, LANES)

time: 195 us -> 192 us (0.985)
  Pallas kernels: 50.8 us -> 48.7 us
where the time goes in v2:
time: 192 us
  blocking collectives  122 us (64%)
  Pallas kernels  48.7 us (25%)
  starting transfers between devices  12.5 us (7%)
  waiting for transfers between devices  5.73 us (3%)
    all_to_all x6, blocking collectives, exchange(): return lax.all_to_all(x, axes, split_axis=0, concat_axis=0, tiled=True)  122 us
    pallas_call x1, Pallas kernels, truncate(): pl.pallas_call(truncate_kernel, out_shape=jax.ShapeDtypeStruct((width, wi...  23.8 us
    ppermute x4, starting transfers between devices, other_core(): return lax.ppermute(x, 'co', [(0, 1), (1, 0)])  12.5 us
    pallas_call x1, Pallas kernels, level_product(): pl.pallas_call(functools.partial(level_gram_kernel, scale), out_shape=(ja...  10.4 us
    pallas_call x1, Pallas kernels, project(): pl.pallas_call(functools.partial(project_kernel, hours), out_shape=(jax.S...  7.27 us
    pallas_call x1, Pallas kernels, hour_gram(): pl.pallas_call(functools.partial(hour_gram_kernel, scale), out_shape=jax....  7.2 us
    ppermute x4, waiting for transfers between devices, other_core(): return lax.ppermute(x, 'co', [(0, 1), (1, 0)])  5.73 us
  transfers between devices with their start and end apart: 4, of which 4 were waited for; matrix products, arithmetic and copies ran while one was open for 0% of the time, Pallas kernels for 0%

profile of v2, /device:TPU:1, one launch (start us, length us, event | category | flops | bytes accessed | tf_op | source)
XLA Modules:
  0.0 191.9 jit_solution(196731716383040578)
XLA Ops:
  0.6 10.4 %level_product.1 = (f32[24,222]{1,0:T(8,128)}, f32[24,222]{1,0:T(8,128)}, bf16[896,4096]{1,0:T(8,128)(2,1)}) custom-call(s32[1]{0:T(128)} %bitcast.core_ref, bf16[222,4,4096]{2,1,0:T(4,128)(2,1)} %bitcast.11, f32[48,222]{1,0:T(8,128)} %bitcast.13), custom_call_target="tpu_custom_call" | custom-call | tf_op jit(solution)/shard_map/level_product/pallas_call | solution.py:213
  11.1 3.3 %collective-permute-start = (f32[24,222]{1,0:T(8,128)}, f32[24,222]{1,0:T(8,128)S(1)}, u32[]{:S(2)}, u32[]{:S(2)}) collective-permute-start(f32[24,222]{1,0:T(8,128)} %get-tuple-element.8), channel_id=1, source_target_pairs={{0,64},{64,0},{1,65},{65,1},{2,66},{66,2},{3,67},{67,3},{4,68},{68... | collective-permute-start | bytes 63944 | tf_op jit(solution)/shard_map/ppermute | solution.py:378
  14.4 1.1 collective-permute-done
  15.5 0.7 add.6
  16.2 14.4 %all_to_all.30 = f32[16,24,222]{2,1,0:T(8,128)S(1)} all-to-all(f32[16,24,222]{2,1,0:T(8,128)S(1)} %broadcast_in_dim.12), channel_id=1, replica_groups=mesh['zl'=2,'co'=2,'y'=4,'zh'=4,'x'=4] {'y','x'}, dimensions={0} | all-to-all | bytes 681984 | tf_op jit(solution)/shard_map/all_to_all | solution.py:382
  30.7 15.4 %all_to_all.31 = f32[8,24,222]{2,1,0:T(8,128)S(1)} all-to-all(f32[8,24,222]{2,1,0:T(8,128)S(1)} %broadcast_in_dim.13), channel_id=1, replica_groups=mesh['zl'=2,'co'=2,'y'=4,'zh'=4,'x'=4] {'zl','zh'}, dimensions={0} | all-to-all | bytes 340992 | tf_op jit(solution)/shard_map/all_to_all | solution.py:382
  46.1 0.0 copy-start.2
  46.1 2.8 %collective-permute-start.1 = (f32[24,222]{1,0:T(8,128)S(1)}, f32[24,222]{1,0:T(8,128)S(1)}, u32[]{:S(2)}, u32[]{:S(2)}) collective-permute-start(f32[24,222]{1,0:T(8,128)S(1)} %reduce_sum.37.mine_ref), channel_id=1, source_target_pairs={{0,64},{64,0},{1,65},{65,1},{2,66},{66,2},{3,67},{67,3},{4,68},{68... | collective-permute-start | bytes 63944 | tf_op jit(solution)/shard_map/ppermute | solution.py:378
  48.8 0.8 collective-permute-done.1.other_ref
  49.7 0.0 copy-start.3
  49.7 0.0 copy-done.2
  49.7 0.6 copy-done.3
  50.3 7.3 %project.1 = (f32[48,222]{1,0:T(8,128)}, bf16[8,32,24,128]{3,2,1,0:T(8,128)(2,1)}) custom-call(s32[1]{0:T(128)} %bitcast.core_ref, f32[24,222]{1,0:T(8,128)} %copy-done.2, f32[24,222]{1,0:T(8,128)} %copy-done.3, bf16[896,4096]{1,0:T(8,128)(2,1)} %get-tuple-element.9.flat_ref), custom_call_target="tpu_custom_call" | custom-call | tf_op jit(solution)/shard_map/project/pallas_call | solution.py:274
  57.6 0.0 copy-start.1
  57.6 46.6 %all_to_all.32.got_ref = bf16[256,24,128]{2,1,0:T(8,128)(2,1)S(1)} all-to-all(bf16[256,24,128]{2,1,0:T(8,128)(2,1)} %bitcast.12), channel_id=1, replica_groups=mesh['zl'=2,'co'=2,'y'=4,'zh'=4,'x'=4] {'zl','co','y','zh','x'}, dimensions={0} | all-to-all | bytes 3145728 | tf_op jit(solution)/shard_map/all_to_all | solution.py:382
  104.2 0.0 copy-done.1
  104.2 7.2 %hour_gram.1 = f32[2,16,24,512]{3,2,1,0:T(8,128)S(1)} custom-call(s32[1]{0:T(128)} %bitcast.core_ref, s32[8]{0:T(128)S(1)} %copy-done.1, bf16[256,24,128]{2,1,0:T(8,128)(2,1)S(1)} %all_to_all.32.got_ref), custom_call_target="tpu_custom_call" | custom-call | tf_op jit(solution)/shard_map/hour_gram/pallas_call | solution.py:358
  111.4 0.1 slice_bitcast_fusion
  111.5 1.2 collective-permute-start.2
  112.7 1.9 collective-permute-done.2
  114.6 0.1 fusion
  114.7 18.5 %all_to_all.33 = f32[16,24,512]{2,1,0:T(8,128)S(1)} all-to-all(f32[16,24,512]{2,1,0:T(8,128)S(1)} %fusion), channel_id=1, replica_groups=mesh['zl'=2,'co'=2,'y'=4,'zh'=4,'x'=4] {'y','x'}, dimensions={0} | all-to-all | bytes 1572864 | tf_op jit(solution)/shard_map/all_to_all | solution.py:382
  133.3 0.1 reduce_sum.38
  133.4 13.6 %all_to_all.34 = f32[8,24,512]{2,1,0:T(8,128)S(1)} all-to-all(f32[8,24,512]{2,1,0:T(8,128)S(1)} %broadcast_in_dim.14), channel_id=1, replica_groups=mesh['zl'=2,'co'=2,'y'=4,'zh'=4,'x'=4] {'zl','zh'}, dimensions={0} | all-to-all | bytes 786432 | tf_op jit(solution)/shard_map/all_to_all | solution.py:382
  147.0 0.0 copy-start
  147.0 0.1 broadcast_in_dim.15
  147.1 13.7 %all_to_all.35.mine_ref = f32[16,24,512]{2,1,0:T(8,128)S(1)} all-to-all(f32[16,24,512]{2,1,0:T(8,128)S(1)} %broadcast_in_dim.15), channel_id=1, replica_groups=mesh['zl'=2,'co'=2,'y'=4,'zh'=4,'x'=4] {'y','x'}, dimensions={0} | all-to-all | bytes 1572864 | tf_op jit(solution)/shard_map/all_to_all | solution.py:382
  160.8 5.3 %collective-permute-start.3 = (f32[16,24,512]{2,1,0:T(8,128)S(1)}, f32[16,24,512]{2,1,0:T(8,128)S(1)}, u32[]{:S(2)}, u32[]{:S(2)}) collective-permute-start(f32[16,24,512]{2,1,0:T(8,128)S(1)} %all_to_all.35.mine_ref), channel_id=1, source_target_pairs={{0,64},{64,0},{1,65},{65,1},{2,66},{66,2},{3,67},{67,3},{4,68},{68... | collective-permute-start | bytes 2359304 | tf_op jit(solution)/shard_map/ppermute | solution.py:378
  166.0 1.9 collective-permute-done.3.other_ref
  168.0 0.0 copy-done
  168.0 23.8 %truncate.1 = f32[768,768]{1,0:T(8,128)} custom-call(s32[1]{0:T(128)} %bitcast.core_ref, f32[16,24,512]{2,1,0:T(8,128)S(1)} %all_to_all.35.mine_ref, f32[16,24,512]{2,1,0:T(8,128)S(1)} %collective-permute-done.3.other_ref, f32[768,128]{1,0:T(8,128)S(1)} %copy-done), custom_call_target="tpu_custom_call" | custom-call | tf_op jit(solution)/shard_map/truncate/pallas_call | solution.py:130
  (6 shorter events, 0.2 us)
Async XLA Ops:
  11.1 4.4 %collective-permute-start = (f32[24,222]{1,0:T(8,128)}, f32[24,222]{1,0:T(8,128)S(1)}, u32[]{:S(2)}, u32[]{:S(2)}) collective-permute-start(f32[24,222]{1,0:T(8,128)} %get-tuple-element.8), channel_id=1, source_target_pairs={{0,64},{64,0},{1,65},{65,1},{2,66},{66,2},{3,67},{67,3},{4,68},{68... | collective-permute-start | bytes 63944 | tf_op jit(solution)/shard_map/ppermute | solution.py:378
  46.1 3.6 %copy-start.2 = (f32[24,222]{1,0:T(8,128)}, f32[24,222]{1,0:T(8,128)S(1)}, u32[]{:S(2)}) copy-start(f32[24,222]{1,0:T(8,128)S(1)} %reduce_sum.37.mine_ref) | copy-start | bytes 63940
  46.1 3.6 %collective-permute-start.1 = (f32[24,222]{1,0:T(8,128)S(1)}, f32[24,222]{1,0:T(8,128)S(1)}, u32[]{:S(2)}, u32[]{:S(2)}) collective-permute-start(f32[24,222]{1,0:T(8,128)S(1)} %reduce_sum.37.mine_ref), channel_id=1, source_target_pairs={{0,64},{64,0},{1,65},{65,1},{2,66},{66,2},{3,67},{67,3},{4,68},{68... | collective-permute-start | bytes 63944 | tf_op jit(solution)/shard_map/ppermute | solution.py:378
  49.7 0.6 copy-start.3
  57.6 46.6 %copy-start.1 = (s32[8]{0:T(128)S(1)}, s32[8]{0:T(128)}, u32[]{:S(2)}) copy-start(s32[8]{0:T(128)} %lag_ref.1) | copy-start | bytes 100
  111.5 3.1 %collective-permute-start.2 = (f32[16,24,512]{2,1,0:T(8,128)S(1)}, f32[16,24,512]{2,1,0:T(8,128)S(1)}, u32[]{:S(2)}, u32[]{:S(2)}) collective-permute-start(f32[16,24,512]{2,1,0:T(8,128)S(1)} %slice_bitcast_fusion), channel_id=1, source_target_pairs={{0,64},{64,0},{1,65},{65,1},{2,66},{66,2},{3,67},{67,3},{4,68},{68... | collective-permute-start | bytes 2359304 | tf_op jit(solution)/shard_map/ppermute | solution.py:378
  147.0 21.0 %copy-start = (f32[768,128]{1,0:T(8,128)S(1)}, f32[768,128]{1,0:T(8,128)}, u32[]{:S(2)}) copy-start(f32[768,128]{1,0:T(8,128)} %start_ref.1) | copy-start | bytes 1179652
  160.8 7.2 %collective-permute-start.3 = (f32[16,24,512]{2,1,0:T(8,128)S(1)}, f32[16,24,512]{2,1,0:T(8,128)S(1)}, u32[]{:S(2)}, u32[]{:S(2)}) collective-permute-start(f32[16,24,512]{2,1,0:T(8,128)S(1)} %all_to_all.35.mine_ref), channel_id=1, source_target_pairs={{0,64},{64,0},{1,65},{65,1},{2,66},{66,2},{3,67},{67,3},{4,68},{68... | collective-permute-start | bytes 2359304 | tf_op jit(solution)/shard_map/ppermute | solution.py:378

commit v3 on v2

--- a/solution.py
+++ b/solution.py
@@ -59,7 +59,17 @@
                 for r in range(k + 1, 8):
                     row[r] = row[r] - low[r, k] * row[k]
             out_ref[8 * here + k : 8 * here + k + 1, :] = side[1][k][0:1, :]
-        for t in range(here + 1, tiles):
+        back = list(side[0]), list(side[1])
+        for row in back:
+            for k in reversed(range(8)):
+                row[k] = row[k] * inv[k]
+                for r in range(k):
+                    row[r] = row[r] - low[k, r] * row[k]
+        for t in range(here + 2, tiles):
+            for k in range(8):
+                left[t] = left[t] - cols[k][t] * back[0][k]
+                right[t] = right[t] - cols[k][t] * back[1][k]
+        for t in range(here + 1, min(here + 2, tiles)):
             mult = [cols[k][t] for k in range(8)]
             for k in range(8):
                 mult[k] = mult[k] * inv[k]
@@ -75,8 +85,8 @@
     for ref, core in ((mine_ref, core_ref[0]), (other_ref, 1 - core_ref[0])):
         for k in range(each):
             half_ref[pl.ds(pl.multiple_of((core * each + k) * high, 8), high), :] = ref[k]
-    for (down, along), (i, j) in stored(width // LANES):
-        block = half_ref[LANES * down : LANES * (down + 1), LANES * along : LANES * (along + 1)]
+    for spot, (i, j) in enumerate(upper(width // LANES)):
+        block = half_ref[LANES * spot : LANES * (spot + 1), :]
         d_ref[LANES * i : LANES * (i + 1), LANES * j : LANES * (j + 1)] = block
         if i != j:
             d_ref[LANES * j : LANES * (j + 1), LANES * i : LANES * (i + 1)] = block.T
@@ -134,7 +144,7 @@
         out_specs=pl.BlockSpec(memory_space=pltpu.HBM),
         scratch_shapes=[
             pltpu.VMEM((width, width), f32),
-            pltpu.VMEM((width, 4 * LANES), f32),
+            pltpu.VMEM((mine.size // LANES * 2, LANES), f32),
             pltpu.VMEM((3, width, width), jnp.bfloat16),
             pltpu.VMEM((rank, width), f32),
             pltpu.VMEM((rank, width), f32),
@@ -286,19 +296,21 @@
             pltpu.VMEM((total, columns), jnp.bfloat16),
             pltpu.SemaphoreType.DMA((4,)),
         ],
-        compiler_params=pltpu.CompilerParams(vmem_limit_bytes=58 * 2**20),
+        compiler_params=pltpu.CompilerParams(vmem_limit_bytes=53 * 2**20),
         name="project",
     )(core, mine, other, flat)
 
 
-def stored(blocks):
-    pairs = [((i, j - i), (i, j)) for i in range(blocks) for j in range(i, min(i + 4, blocks))]
-    return pairs + [((3, 3), (0, 4)), ((4, 2), (0, 5)), ((4, 3), (1, 5))]
-
-
-def hour_gram_kernel(scale, core_ref, lag_ref, got_ref, out_ref, flat_ref, gram_ref, half_ref):
+def upper(blocks):
+    return [(i, j) for i in range(blocks) for j in range(i, blocks)]
+
+
+def piece_rows(blocks):
+    return -(-len(upper(blocks)) * LANES // (32 * 8)) * 8
+
+
+def hour_gram_kernel(scale, blocks, core_ref, lag_ref, got_ref, out_ref, flat_ref, gram_ref, half_ref):
     senders, rows, _ = got_ref.shape
-    width = half_ref.shape[0]
     f32, bf16 = jnp.float32, jnp.bfloat16
     hours = flat_ref.shape[0] // senders
     per = rows // hours
@@ -323,12 +335,12 @@
         for b in range(first // LANES, gram_ref.shape[0]):
             gram_ref[b, i : i + 256, :] = band[:, LANES * b - first : LANES * (b + 1) - first]
 
-    blocks, some = width // LANES, 32
+    some = 32
     lane = lax.broadcasted_iota(jnp.int32, (some, LANES), 1)
     lags = [lag_ref[j] for j in range(lag_ref.shape[0])]
     whole = [lax.div(offset, LANES) for offset in lags]
     part = [lax.rem(offset, LANES) for offset in lags]
-    spots = {pair: spot for spot, pair in stored(blocks)}
+    spots = {pair: spot for spot, pair in enumerate(upper(blocks))}
     for i in range(blocks):
         for r in range(0, LANES, some):
             acc = {b: jnp.zeros((some, LANES), f32) for b in range(i, blocks)}
@@ -340,9 +352,10 @@
                     load[b] = pltpu.roll(block, lax.rem(LANES - part[j], LANES), 1)
                 acc = {b: acc[b] + jnp.where(lane < LANES - part[j], load[b], load[b + 1]) for b in acc}
             for b in acc:
-                down, along = spots[i, b]
-                half_ref[LANES * down + r : LANES * down + r + some, LANES * along : LANES * (along + 1)] = acc[b] * scale
-    half_ref[width - LANES :, LANES:] = jnp.zeros((LANES, half_ref.shape[1] - LANES), f32)
+                at = LANES * spots[i, b] + r
+                half_ref[at : at + some, :] = acc[b] * scale
+    made = LANES * len(spots)
+    half_ref[made:, :] = jnp.zeros((half_ref.shape[0] - made, LANES), f32)
     _, each, high, _ = out_ref.shape
     for c in range(2):
         for k in range(each):
@@ -353,17 +366,18 @@
 def hour_gram(core, lags, got, width, hours, scale):
     senders, rows, _ = got.shape
     total = senders * hours
-    wide = 4 * LANES
+    blocks = width // LANES
+    high = piece_rows(blocks)
     smem, vm = pl.BlockSpec(memory_space=pltpu.SMEM), pl.BlockSpec(memory_space=pltpu.VMEM)
     return pl.pallas_call(
-        functools.partial(hour_gram_kernel, scale),
-        out_shape=jax.ShapeDtypeStruct((2, 16, width // 32, wide), jnp.float32),
+        functools.partial(hour_gram_kernel, scale, blocks),
+        out_shape=jax.ShapeDtypeStruct((2, 16, high, LANES), jnp.float32),
         in_specs=[smem, smem, vm],
         out_specs=vm,
         scratch_shapes=[
             pltpu.VMEM((total, rows // hours * LANES), jnp.bfloat16),
             pltpu.VMEM((total // LANES, total, LANES), jnp.float32),
-            pltpu.VMEM((width, wide), jnp.float32),
+            pltpu.VMEM((32 * high, LANES), jnp.float32),
         ],
         compiler_params=pltpu.CompilerParams(vmem_limit_bytes=48 * 2**20),
         name="hour_gram",

time: 192 us -> 189 us (0.984)
  no operation moved by 1% of the time
where the time goes in v3:
time: 189 us; the launch traced here: 188 us
  blocking collectives  121 us (64%)
  Pallas kernels  47.5 us (25%)
  starting transfers between devices  11.9 us (6%)
  waiting for transfers between devices  5.55 us (3%)
    all_to_all x6, blocking collectives, exchange(): return lax.all_to_all(x, axes, split_axis=0, concat_axis=0, tiled=True)  121 us
    pallas_call x1, Pallas kernels, truncate(): pl.pallas_call(truncate_kernel, out_shape=jax.ShapeDtypeStruct((width, wi...  23.4 us
    ppermute x4, starting transfers between devices, other_core(): return lax.ppermute(x, 'co', [(0, 1), (1, 0)])  11.9 us
    pallas_call x1, Pallas kernels, level_product(): pl.pallas_call(functools.partial(level_gram_kernel, scale), out_shape=(ja...  10.4 us
    pallas_call x1, Pallas kernels, hour_gram(): pl.pallas_call(functools.partial(hour_gram_kernel, scale, blocks), out_sh...  7.14 us
    pallas_call x1, Pallas kernels, project(): pl.pallas_call(functools.partial(project_kernel, hours), out_shape=(jax.S...  6.57 us
    ppermute x4, waiting for transfers between devices, other_core(): return lax.ppermute(x, 'co', [(0, 1), (1, 0)])  5.55 us
  transfers between devices with their start and end apart: 4, of which 4 were waited for; matrix products, arithmetic and copies ran while one was open for 0% of the time, Pallas kernels for 0%

profile of v3, /device:TPU:1, one launch (start us, length us, event | category | flops | bytes accessed | tf_op | source)
XLA Modules:
  0.0 188.5 jit_solution(8982523734347215378)
XLA Ops:
  0.6 10.4 %level_product.1 = (f32[24,222]{1,0:T(8,128)}, f32[24,222]{1,0:T(8,128)}, bf16[896,4096]{1,0:T(8,128)(2,1)}) custom-call(s32[1]{0:T(128)} %bitcast.core_ref, bf16[222,4,4096]{2,1,0:T(4,128)(2,1)} %bitcast.11, f32[48,222]{1,0:T(8,128)} %bitcast.13), custom_call_target="tpu_custom_call" | custom-call | tf_op jit(solution)/shard_map/level_product/pallas_call | solution.py:223
  11.1 3.3 %collective-permute-start = (f32[24,222]{1,0:T(8,128)}, f32[24,222]{1,0:T(8,128)S(1)}, u32[]{:S(2)}, u32[]{:S(2)}) collective-permute-start(f32[24,222]{1,0:T(8,128)} %get-tuple-element.8), channel_id=1, source_target_pairs={{0,64},{64,0},{1,65},{65,1},{2,66},{66,2},{3,67},{67,3},{4,68},{68... | collective-permute-start | bytes 63944 | tf_op jit(solution)/shard_map/ppermute | solution.py:392
  14.4 1.1 collective-permute-done
  15.5 0.7 add.6
  16.2 14.4 %all_to_all.30 = f32[16,24,222]{2,1,0:T(8,128)S(1)} all-to-all(f32[16,24,222]{2,1,0:T(8,128)S(1)} %broadcast_in_dim.12), channel_id=1, replica_groups=mesh['zl'=2,'co'=2,'y'=4,'zh'=4,'x'=4] {'y','x'}, dimensions={0} | all-to-all | bytes 681984 | tf_op jit(solution)/shard_map/all_to_all | solution.py:396
  30.7 15.4 %all_to_all.31 = f32[8,24,222]{2,1,0:T(8,128)S(1)} all-to-all(f32[8,24,222]{2,1,0:T(8,128)S(1)} %broadcast_in_dim.13), channel_id=1, replica_groups=mesh['zl'=2,'co'=2,'y'=4,'zh'=4,'x'=4] {'zl','zh'}, dimensions={0} | all-to-all | bytes 340992 | tf_op jit(solution)/shard_map/all_to_all | solution.py:396
  46.1 2.8 %collective-permute-start.1 = (f32[24,222]{1,0:T(8,128)S(1)}, f32[24,222]{1,0:T(8,128)S(1)}, u32[]{:S(2)}, u32[]{:S(2)}) collective-permute-start(f32[24,222]{1,0:T(8,128)S(1)} %reduce_sum.37.mine_ref), channel_id=1, source_target_pairs={{0,64},{64,0},{1,65},{65,1},{2,66},{66,2},{3,67},{67,3},{4,68},{68... | collective-permute-start | bytes 63944 | tf_op jit(solution)/shard_map/ppermute | solution.py:392
  48.8 0.8 collective-permute-done.1.other_ref
  49.7 6.6 %project.1 = (f32[48,222]{1,0:T(8,128)}, bf16[8,32,24,128]{3,2,1,0:T(8,128)(2,1)}) custom-call(s32[1]{0:T(128)} %bitcast.core_ref, f32[24,222]{1,0:T(8,128)S(1)} %reduce_sum.37.mine_ref, f32[24,222]{1,0:T(8,128)S(1)} %collective-permute-done.1.other_ref, bf16[896,4096]{1,0:T(8,128)(2,1)} %get-tuple-element.9.flat_ref), custom_call_target="tpu_custom_call" | custom-call | tf_op jit(solution)/shard_map/project/pallas_call | solution.py:284
  56.3 0.0 copy-start.1
  56.3 46.6 %all_to_all.32.got_ref = bf16[256,24,128]{2,1,0:T(8,128)(2,1)S(1)} all-to-all(bf16[256,24,128]{2,1,0:T(8,128)(2,1)} %bitcast.12), channel_id=1, replica_groups=mesh['zl'=2,'co'=2,'y'=4,'zh'=4,'x'=4] {'zl','co','y','zh','x'}, dimensions={0} | all-to-all | bytes 3145728 | tf_op jit(solution)/shard_map/all_to_all | solution.py:396
  102.9 0.0 copy-done.1
  102.9 7.1 %hour_gram.1 = f32[2,16,88,128]{3,2,1,0:T(8,128)S(1)} custom-call(s32[1]{0:T(128)} %bitcast.core_ref, s32[8]{0:T(128)S(1)} %copy-done.1, bf16[256,24,128]{2,1,0:T(8,128)(2,1)S(1)} %all_to_all.32.got_ref), custom_call_target="tpu_custom_call" | custom-call | tf_op jit(solution)/shard_map/hour_gram/pallas_call | solution.py:372
  110.1 1.2 collective-permute-start.2
  111.3 1.8 collective-permute-done.2
  113.1 0.1 fusion
  113.2 17.8 %all_to_all.33 = f32[16,88,128]{2,1,0:T(8,128)S(1)} all-to-all(f32[16,88,128]{2,1,0:T(8,128)S(1)} %fusion), channel_id=1, replica_groups=mesh['zl'=2,'co'=2,'y'=4,'zh'=4,'x'=4] {'y','x'}, dimensions={0} | all-to-all | bytes 1441792 | tf_op jit(solution)/shard_map/all_to_all | solution.py:396
  131.1 0.0 copy-start
  131.1 13.7 %all_to_all.34 = f32[8,88,128]{2,1,0:T(8,128)S(1)} all-to-all(f32[8,88,128]{2,1,0:T(8,128)S(1)} %broadcast_in_dim.14), channel_id=1, replica_groups=mesh['zl'=2,'co'=2,'y'=4,'zh'=4,'x'=4] {'zl','zh'}, dimensions={0} | all-to-all | bytes 720896 | tf_op jit(solution)/shard_map/all_to_all | solution.py:396
  144.9 13.6 %all_to_all.35.mine_ref = f32[16,88,128]{2,1,0:T(8,128)S(1)} all-to-all(f32[16,88,128]{2,1,0:T(8,128)S(1)} %broadcast_in_dim.15), channel_id=1, replica_groups=mesh['zl'=2,'co'=2,'y'=4,'zh'=4,'x'=4] {'y','x'}, dimensions={0} | all-to-all | bytes 1441792 | tf_op jit(solution)/shard_map/all_to_all | solution.py:396
  158.5 4.6 %collective-permute-start.3 = (f32[16,88,128]{2,1,0:T(8,128)S(1)}, f32[16,88,128]{2,1,0:T(8,128)S(1)}, u32[]{:S(2)}, u32[]{:S(2)}) collective-permute-start(f32[16,88,128]{2,1,0:T(8,128)S(1)} %all_to_all.35.mine_ref), channel_id=1, source_target_pairs={{0,64},{64,0},{1,65},{65,1},{2,66},{66,2},{3,67},{67,3},{4,68},{68... | collective-permute-start | bytes 2162696 | tf_op jit(solution)/shard_map/ppermute | solution.py:392
  163.1 1.8 collective-permute-done.3.other_ref
  164.9 0.0 copy-done
  164.9 23.4 %truncate.1 = f32[768,768]{1,0:T(8,128)} custom-call(s32[1]{0:T(128)} %bitcast.core_ref, f32[16,88,128]{2,1,0:T(8,128)S(1)} %all_to_all.35.mine_ref, f32[16,88,128]{2,1,0:T(8,128)S(1)} %collective-permute-done.3.other_ref, f32[768,128]{1,0:T(8,128)S(1)} %copy-done), custom_call_target="tpu_custom_call" | custom-call | tf_op jit(solution)/shard_map/truncate/pallas_call | solution.py:140
  (9 shorter events, 0.3 us)
Async XLA Ops:
  11.1 4.4 %collective-permute-start = (f32[24,222]{1,0:T(8,128)}, f32[24,222]{1,0:T(8,128)S(1)}, u32[]{:S(2)}, u32[]{:S(2)}) collective-permute-start(f32[24,222]{1,0:T(8,128)} %get-tuple-element.8), channel_id=1, source_target_pairs={{0,64},{64,0},{1,65},{65,1},{2,66},{66,2},{3,67},{67,3},{4,68},{68... | collective-permute-start | bytes 63944 | tf_op jit(solution)/shard_map/ppermute | solution.py:392
  46.1 3.6 %collective-permute-start.1 = (f32[24,222]{1,0:T(8,128)S(1)}, f32[24,222]{1,0:T(8,128)S(1)}, u32[]{:S(2)}, u32[]{:S(2)}) collective-permute-start(f32[24,222]{1,0:T(8,128)S(1)} %reduce_sum.37.mine_ref), channel_id=1, source_target_pairs={{0,64},{64,0},{1,65},{65,1},{2,66},{66,2},{3,67},{67,3},{4,68},{68... | collective-permute-start | bytes 63944 | tf_op jit(solution)/shard_map/ppermute | solution.py:392
  56.3 46.7 %copy-start.1 = (s32[8]{0:T(128)S(1)}, s32[8]{0:T(128)}, u32[]{:S(2)}) copy-start(s32[8]{0:T(128)} %lag_ref.1) | copy-start | bytes 100
  110.1 3.0 %collective-permute-start.2 = (f32[16,88,128]{2,1,0:T(8,128)S(1)}, f32[16,88,128]{2,1,0:T(8,128)S(1)}, u32[]{:S(2)}, u32[]{:S(2)}) collective-permute-start(f32[16,88,128]{2,1,0:T(8,128)S(1)} %slice_bitcast_fusion), channel_id=1, source_target_pairs={{0,64},{64,0},{1,65},{65,1},{2,66},{66,2},{3,67},{67,3},{4,68},{68... | collective-permute-start | bytes 2162696 | tf_op jit(solution)/shard_map/ppermute | solution.py:392
  131.1 33.8 %copy-start = (f32[768,128]{1,0:T(8,128)S(1)}, f32[768,128]{1,0:T(8,128)}, u32[]{:S(2)}) copy-start(f32[768,128]{1,0:T(8,128)} %start_ref.1) | copy-start | bytes 1179652
  158.5 6.4 %collective-permute-start.3 = (f32[16,88,128]{2,1,0:T(8,128)S(1)}, f32[16,88,128]{2,1,0:T(8,128)S(1)}, u32[]{:S(2)}, u32[]{:S(2)}) collective-permute-start(f32[16,88,128]{2,1,0:T(8,128)S(1)} %all_to_all.35.mine_ref), channel_id=1, source_target_pairs={{0,64},{64,0},{1,65},{65,1},{2,66},{66,2},{3,67},{67,3},{4,68},{68... | collective-permute-start | bytes 2162696 | tf_op jit(solution)/shard_map/ppermute | solution.py:392

commit v4 on v3

--- a/solution.py
+++ b/solution.py
@@ -335,7 +335,7 @@
         for b in range(first // LANES, gram_ref.shape[0]):
             gram_ref[b, i : i + 256, :] = band[:, LANES * b - first : LANES * (b + 1) - first]
 
-    some = 32
+    some = 16
     lane = lax.broadcasted_iota(jnp.int32, (some, LANES), 1)
     lags = [lag_ref[j] for j in range(lag_ref.shape[0])]
     whole = [lax.div(offset, LANES) for offset in lags]

time: 189 us -> 189 us (level)
  no operation moved by 1% of the time
where the time goes in v4:
time: 189 us; the launch traced here: 188 us
  blocking collectives  121 us (64%)
  Pallas kernels  47.5 us (25%)
  starting transfers between devices  11.9 us (6%)
  waiting for transfers between devices  5.55 us (3%)
    all_to_all x6, blocking collectives, exchange(): return lax.all_to_all(x, axes, split_axis=0, concat_axis=0, tiled=True)  121 us
    pallas_call x1, Pallas kernels, truncate(): pl.pallas_call(truncate_kernel, out_shape=jax.ShapeDtypeStruct((width, wi...  23.4 us
    ppermute x4, starting transfers between devices, other_core(): return lax.ppermute(x, 'co', [(0, 1), (1, 0)])  11.9 us
    pallas_call x1, Pallas kernels, level_product(): pl.pallas_call(functools.partial(level_gram_kernel, scale), out_shape=(ja...  10.4 us
    pallas_call x1, Pallas kernels, hour_gram(): pl.pallas_call(functools.partial(hour_gram_kernel, scale, blocks), out_sh...  7.07 us
    pallas_call x1, Pallas kernels, project(): pl.pallas_call(functools.partial(project_kernel, hours), out_shape=(jax.S...  6.57 us
    ppermute x4, waiting for transfers between devices, other_core(): return lax.ppermute(x, 'co', [(0, 1), (1, 0)])  5.55 us
  transfers between devices with their start and end apart: 4, of which 4 were waited for; matrix products, arithmetic and copies ran while one was open for 0% of the time, Pallas kernels for 0%

profile of v4, /device:TPU:1, one launch (start us, length us, event | category | flops | bytes accessed | tf_op | source)
XLA Modules:
  0.0 188.4 jit_solution(16708868425779191866)
XLA Ops:
  0.6 10.4 %level_product.1 = (f32[24,222]{1,0:T(8,128)}, f32[24,222]{1,0:T(8,128)}, bf16[896,4096]{1,0:T(8,128)(2,1)}) custom-call(s32[1]{0:T(128)} %bitcast.core_ref, bf16[222,4,4096]{2,1,0:T(4,128)(2,1)} %bitcast.11, f32[48,222]{1,0:T(8,128)} %bitcast.13), custom_call_target="tpu_custom_call" | custom-call | tf_op jit(solution)/shard_map/level_product/pallas_call | solution.py:223
  11.1 3.3 %collective-permute-start = (f32[24,222]{1,0:T(8,128)}, f32[24,222]{1,0:T(8,128)S(1)}, u32[]{:S(2)}, u32[]{:S(2)}) collective-permute-start(f32[24,222]{1,0:T(8,128)} %get-tuple-element.8), channel_id=1, source_target_pairs={{0,64},{64,0},{1,65},{65,1},{2,66},{66,2},{3,67},{67,3},{4,68},{68... | collective-permute-start | bytes 63944 | tf_op jit(solution)/shard_map/ppermute | solution.py:392
  14.4 1.1 collective-permute-done
  15.5 0.7 add.6
  16.2 14.4 %all_to_all.30 = f32[16,24,222]{2,1,0:T(8,128)S(1)} all-to-all(f32[16,24,222]{2,1,0:T(8,128)S(1)} %broadcast_in_dim.12), channel_id=1, replica_groups=mesh['zl'=2,'co'=2,'y'=4,'zh'=4,'x'=4] {'y','x'}, dimensions={0} | all-to-all | bytes 681984 | tf_op jit(solution)/shard_map/all_to_all | solution.py:396
  30.7 15.4 %all_to_all.31 = f32[8,24,222]{2,1,0:T(8,128)S(1)} all-to-all(f32[8,24,222]{2,1,0:T(8,128)S(1)} %broadcast_in_dim.13), channel_id=1, replica_groups=mesh['zl'=2,'co'=2,'y'=4,'zh'=4,'x'=4] {'zl','zh'}, dimensions={0} | all-to-all | bytes 340992 | tf_op jit(solution)/shard_map/all_to_all | solution.py:396
  46.1 2.8 %collective-permute-start.1 = (f32[24,222]{1,0:T(8,128)S(1)}, f32[24,222]{1,0:T(8,128)S(1)}, u32[]{:S(2)}, u32[]{:S(2)}) collective-permute-start(f32[24,222]{1,0:T(8,128)S(1)} %reduce_sum.37.mine_ref), channel_id=1, source_target_pairs={{0,64},{64,0},{1,65},{65,1},{2,66},{66,2},{3,67},{67,3},{4,68},{68... | collective-permute-start | bytes 63944 | tf_op jit(solution)/shard_map/ppermute | solution.py:392
  48.8 0.8 collective-permute-done.1.other_ref
  49.7 6.6 %project.1 = (f32[48,222]{1,0:T(8,128)}, bf16[8,32,24,128]{3,2,1,0:T(8,128)(2,1)}) custom-call(s32[1]{0:T(128)} %bitcast.core_ref, f32[24,222]{1,0:T(8,128)S(1)} %reduce_sum.37.mine_ref, f32[24,222]{1,0:T(8,128)S(1)} %collective-permute-done.1.other_ref, bf16[896,4096]{1,0:T(8,128)(2,1)} %get-tuple-element.9.flat_ref), custom_call_target="tpu_custom_call" | custom-call | tf_op jit(solution)/shard_map/project/pallas_call | solution.py:284
  56.3 0.0 copy-start.1
  56.3 46.6 %all_to_all.32.got_ref = bf16[256,24,128]{2,1,0:T(8,128)(2,1)S(1)} all-to-all(bf16[256,24,128]{2,1,0:T(8,128)(2,1)} %bitcast.12), channel_id=1, replica_groups=mesh['zl'=2,'co'=2,'y'=4,'zh'=4,'x'=4] {'zl','co','y','zh','x'}, dimensions={0} | all-to-all | bytes 3145728 | tf_op jit(solution)/shard_map/all_to_all | solution.py:396
  102.9 0.0 copy-done.1
  102.9 7.1 %hour_gram.1 = f32[2,16,88,128]{3,2,1,0:T(8,128)S(1)} custom-call(s32[1]{0:T(128)} %bitcast.core_ref, s32[8]{0:T(128)S(1)} %copy-done.1, bf16[256,24,128]{2,1,0:T(8,128)(2,1)S(1)} %all_to_all.32.got_ref), custom_call_target="tpu_custom_call" | custom-call | tf_op jit(solution)/shard_map/hour_gram/pallas_call | solution.py:372
  110.0 1.2 collective-permute-start.2
  111.2 1.8 collective-permute-done.2
  113.1 0.1 fusion
  113.1 17.8 %all_to_all.33 = f32[16,88,128]{2,1,0:T(8,128)S(1)} all-to-all(f32[16,88,128]{2,1,0:T(8,128)S(1)} %fusion), channel_id=1, replica_groups=mesh['zl'=2,'co'=2,'y'=4,'zh'=4,'x'=4] {'y','x'}, dimensions={0} | all-to-all | bytes 1441792 | tf_op jit(solution)/shard_map/all_to_all | solution.py:396
  131.1 0.0 copy-start
  131.1 13.7 %all_to_all.34 = f32[8,88,128]{2,1,0:T(8,128)S(1)} all-to-all(f32[8,88,128]{2,1,0:T(8,128)S(1)} %broadcast_in_dim.14), channel_id=1, replica_groups=mesh['zl'=2,'co'=2,'y'=4,'zh'=4,'x'=4] {'zl','zh'}, dimensions={0} | all-to-all | bytes 720896 | tf_op jit(solution)/shard_map/all_to_all | solution.py:396
  144.9 13.6 %all_to_all.35.mine_ref = f32[16,88,128]{2,1,0:T(8,128)S(1)} all-to-all(f32[16,88,128]{2,1,0:T(8,128)S(1)} %broadcast_in_dim.15), channel_id=1, replica_groups=mesh['zl'=2,'co'=2,'y'=4,'zh'=4,'x'=4] {'y','x'}, dimensions={0} | all-to-all | bytes 1441792 | tf_op jit(solution)/shard_map/all_to_all | solution.py:396
  158.4 4.6 %collective-permute-start.3 = (f32[16,88,128]{2,1,0:T(8,128)S(1)}, f32[16,88,128]{2,1,0:T(8,128)S(1)}, u32[]{:S(2)}, u32[]{:S(2)}) collective-permute-start(f32[16,88,128]{2,1,0:T(8,128)S(1)} %all_to_all.35.mine_ref), channel_id=1, source_target_pairs={{0,64},{64,0},{1,65},{65,1},{2,66},{66,2},{3,67},{67,3},{4,68},{68... | collective-permute-start | bytes 2162696 | tf_op jit(solution)/shard_map/ppermute | solution.py:392
  163.0 1.8 collective-permute-done.3.other_ref
  164.8 0.0 copy-done
  164.8 23.4 %truncate.1 = f32[768,768]{1,0:T(8,128)} custom-call(s32[1]{0:T(128)} %bitcast.core_ref, f32[16,88,128]{2,1,0:T(8,128)S(1)} %all_to_all.35.mine_ref, f32[16,88,128]{2,1,0:T(8,128)S(1)} %collective-permute-done.3.other_ref, f32[768,128]{1,0:T(8,128)S(1)} %copy-done), custom_call_target="tpu_custom_call" | custom-call | tf_op jit(solution)/shard_map/truncate/pallas_call | solution.py:140
  (9 shorter events, 0.3 us)
Async XLA Ops:
  11.1 4.4 %collective-permute-start = (f32[24,222]{1,0:T(8,128)}, f32[24,222]{1,0:T(8,128)S(1)}, u32[]{:S(2)}, u32[]{:S(2)}) collective-permute-start(f32[24,222]{1,0:T(8,128)} %get-tuple-element.8), channel_id=1, source_target_pairs={{0,64},{64,0},{1,65},{65,1},{2,66},{66,2},{3,67},{67,3},{4,68},{68... | collective-permute-start | bytes 63944 | tf_op jit(solution)/shard_map/ppermute | solution.py:392
  46.1 3.6 %collective-permute-start.1 = (f32[24,222]{1,0:T(8,128)S(1)}, f32[24,222]{1,0:T(8,128)S(1)}, u32[]{:S(2)}, u32[]{:S(2)}) collective-permute-start(f32[24,222]{1,0:T(8,128)S(1)} %reduce_sum.37.mine_ref), channel_id=1, source_target_pairs={{0,64},{64,0},{1,65},{65,1},{2,66},{66,2},{3,67},{67,3},{4,68},{68... | collective-permute-start | bytes 63944 | tf_op jit(solution)/shard_map/ppermute | solution.py:392
  56.3 46.7 %copy-start.1 = (s32[8]{0:T(128)S(1)}, s32[8]{0:T(128)}, u32[]{:S(2)}) copy-start(s32[8]{0:T(128)} %lag_ref.1) | copy-start | bytes 100
  110.0 3.0 %collective-permute-start.2 = (f32[16,88,128]{2,1,0:T(8,128)S(1)}, f32[16,88,128]{2,1,0:T(8,128)S(1)}, u32[]{:S(2)}, u32[]{:S(2)}) collective-permute-start(f32[16,88,128]{2,1,0:T(8,128)S(1)} %slice_bitcast_fusion), channel_id=1, source_target_pairs={{0,64},{64,0},{1,65},{65,1},{2,66},{66,2},{3,67},{67,3},{4,68},{68... | collective-permute-start | bytes 2162696 | tf_op jit(solution)/shard_map/ppermute | solution.py:392
  131.1 33.8 %copy-start = (f32[768,128]{1,0:T(8,128)S(1)}, f32[768,128]{1,0:T(8,128)}, u32[]{:S(2)}) copy-start(f32[768,128]{1,0:T(8,128)} %start_ref.1) | copy-start | bytes 1179652
  158.4 6.4 %collective-permute-start.3 = (f32[16,88,128]{2,1,0:T(8,128)S(1)}, f32[16,88,128]{2,1,0:T(8,128)S(1)}, u32[]{:S(2)}, u32[]{:S(2)}) collective-permute-start(f32[16,88,128]{2,1,0:T(8,128)S(1)} %all_to_all.35.mine_ref), channel_id=1, source_target_pairs={{0,64},{64,0},{1,65},{65,1},{2,66},{66,2},{3,67},{67,3},{4,68},{68... | collective-permute-start | bytes 2162696 | tf_op jit(solution)/shard_map/ppermute | solution.py:392
